TPU v7x, 1024 devices: a whole 8x8x8 slice. The times are simulated.
1024 devices in a mesh: gx: 64 (over y, z), gy: 16 (over x, core).
Axes of the slice: x: 8, y: 8, z: 8, core: 2. Of those that a mesh axis runs over, the one named last changes fastest.
Arguments:
- old_boxes: float32 [64, 16, 16, 5, 512], P('gx', 'gy'), may hold values from -1 to 5.75, as said below
- send_slot: int32 [64, 16, 16, 2], P('gx', 'gy'), may hold values from 0 to 16, as said below
- arrival: int32 [64, 16, 8], P('gx', 'gy'), may hold values from 0 to 31, as said below
- coarse: float32 [64, 16, 5, 800], P('gx', 'gy'), may hold values from -1 to 5.75, as said below
- coarse_flux: float32 [64, 16, 5, 256], P('gx', 'gy'), may hold values from -6 to 6
Outputs:
- fine_out: float32 [64, 16, 8, 5, 512], P('gx', 'gy')
- coarse_out: float32 [64, 16, 5, 800], P('gx', 'gy')
Inputs may be any that keep to these rules, and one draw needn't show every extreme that they name: Within each segment, send_slot[g, s, d, c] is the old slot of source s holding the c-th box that s sends to d, or 16 where s sends nothing to d; a pair carries 2 boxes or none; no old slot is sent twice; every destination receives exactly 8 boxes; old slots never named hold no box. arrival[g, d, k] = s * 2 + c names the c-th box that s sends to d, which becomes box k of d; every box sent to d is named once. `old_boxes`: every slot holds the conserved fields of a state with density and pressure in [0.5, 2] and velocity components in [-0.5, 0.5]. `coarse`: every cell holds the conserved fields of a state with density and pressure in [0.5, 2] and velocity components in [-0.5, 0.5].
All inputs are finite; a program needn't handle non-finite values.
Results may differ from a plain program's by a relative error of at most 0.0003.
Values sent between devices are 32-bit elements; how exact they have to be, the bound alone decides.
No kernel may reach another device: no remote copies, remote signals or barrier semaphores. Data moves between devices by JAX's collectives and lax.ppermute only.
A program may use at most 32 MiB of HBM per device.

v0:
```python
import jax
import jax.numpy as jnp
from jax import lax
from jax.sharding import PartitionSpec as P

NF = 5
BXY = 16
BZ = 2


GAMMA = 1.4
STEP_RATIO = 0.1


def padded_2(value, sides, width):
    for axis, dim in sides:
        size, length = (lax.axis_size(axis), value.shape[dim])
        up = [(i, (i + 1) % size) for i in range(size)]
        down = [(j, i) for i, j in up]
        last = lax.slice_in_dim(value, length - width, length, axis=dim)
        first = lax.slice_in_dim(value, 0, width, axis=dim)
        before = lax.ppermute(last, axis, up)
        after = lax.ppermute(first, axis, down)
        value = jnp.concatenate([before, value, after], axis=dim)
    return value


def passed_along(value, axis, steps):
    count = lax.axis_size(axis)
    pairs = [(source, (source + steps) % count) for source in range(count)]
    return lax.ppermute(value, axis, pairs)


def primitive(fields):
    density = fields[0]
    velocity = fields[1:4] / density
    pressure = (GAMMA - 1.0) * (fields[4] - 0.5 * density * jnp.sum(velocity * velocity, axis=0))
    return jnp.concatenate([density[None], velocity, pressure[None]], axis=0)


def minmod(first_delta, second_delta):
    return (
        0.5
        * (jnp.sign(first_delta) + jnp.sign(second_delta))
        * jnp.minimum(jnp.abs(first_delta), jnp.abs(second_delta))
    )


def conserved_flux(primitives, component):
    density = primitives[0]
    velocity = primitives[1:4]
    pressure = primitives[4]
    normal = velocity[component - 1]
    energy = pressure / (GAMMA - 1.0) + 0.5 * density * jnp.sum(velocity * velocity, axis=0)
    conserved = jnp.concatenate([density[None], density * velocity, energy[None]], axis=0)
    momentum_flux = density * normal * velocity
    momentum_flux = momentum_flux.at[component - 1].add(pressure)
    flux_all = jnp.concatenate(
        [(density * normal)[None], momentum_flux, ((energy + pressure) * normal)[None]], axis=0
    )
    wave_speed = jnp.abs(normal) + jnp.sqrt(GAMMA * pressure / density)
    return (conserved, flux_all, wave_speed)


def face_flux(padded, axis_index, component):
    length = padded.shape[axis_index]
    interior = length - 4
    deltas = lax.slice_in_dim(padded, 1, length, axis=axis_index) - lax.slice_in_dim(
        padded, 0, length - 1, axis=axis_index
    )
    slopes = minmod(
        lax.slice_in_dim(deltas, 0, length - 2, axis=axis_index),
        lax.slice_in_dim(deltas, 1, length - 1, axis=axis_index),
    )
    lower_state = lax.slice_in_dim(
        padded, 1, interior + 2, axis=axis_index
    ) + 0.5 * lax.slice_in_dim(slopes, 0, interior + 1, axis=axis_index)
    upper_state = lax.slice_in_dim(
        padded, 2, interior + 3, axis=axis_index
    ) - 0.5 * lax.slice_in_dim(slopes, 1, interior + 2, axis=axis_index)
    cons_lower, flux_lower, speed_lower = conserved_flux(lower_state, component)
    cons_upper, flux_upper, speed_upper = conserved_flux(upper_state, component)
    return 0.5 * (flux_lower + flux_upper) - 0.5 * jnp.maximum(speed_lower, speed_upper) * (
        cons_upper - cons_lower
    )


def cycle_faces(coarse_block):
    return jnp.stack(
        [
            coarse_block[:, :, 1:-1, 0],
            coarse_block[:, :, 1:-1, -1],
            coarse_block[:, :, 0, 1:-1],
            coarse_block[:, :, -1, 1:-1],
        ],
        axis=2,
    )


def expand(coarse_faces):
    widened = jnp.repeat(jnp.repeat(coarse_faces, 2, axis=1), 2, axis=3)
    return jnp.broadcast_to(widened[:, :, :, None, :], widened.shape[:3] + (2, widened.shape[3]))


def advance(fields, primitives, lower_rim, upper_rim, ghosts_all):
    prim_z = jnp.concatenate([primitive(lower_rim), primitives, primitive(upper_rim)], axis=1)
    ghost_prim = primitive(ghosts_all)
    prim_y = jnp.concatenate([ghost_prim[:, :, 2], primitives, ghost_prim[:, :, 3]], axis=2)
    prim_x = jnp.concatenate(
        [
            jnp.swapaxes(ghost_prim[:, :, 0], 2, 3),
            primitives,
            jnp.swapaxes(ghost_prim[:, :, 1], 2, 3),
        ],
        axis=3,
    )
    flux_z = face_flux(prim_z, 1, 3)
    flux_y = face_flux(prim_y, 2, 2)
    flux_x = face_flux(prim_x, 3, 1)
    change = (
        flux_z[:, 1:]
        - flux_z[:, :-1]
        + (flux_y[:, :, 1:] - flux_y[:, :, :-1])
        + (flux_x[..., 1:] - flux_x[..., :-1])
    )
    new_fields = fields - STEP_RATIO * change
    side_flux = jnp.stack(
        [flux_x[..., 0], flux_x[..., -1], flux_y[:, :, 0, :], flux_y[:, :, -1, :]], axis=2
    )
    return (new_fields, side_flux)


def restrict(new_fields, side_flux):
    layers = new_fields.shape[1] // 2
    half_edge = BXY // 2
    face_mean = side_flux.reshape(NF, layers, 2, 4, half_edge, 2).mean(axis=(2, 5))
    averaged = new_fields.reshape(NF, layers, 2, half_edge, 2, half_edge, 2).mean(axis=(2, 4, 6))
    return (face_mean, averaged)


def coarse_update(coarse_block, face_mean, averaged, register):
    signs = jnp.array([-1.0, 1.0, -1.0, 1.0], dtype=coarse_block.dtype)
    correction = 0.5 * STEP_RATIO * (face_mean - register) * signs[None, None, :, None]
    new_block = coarse_block.at[:, :, 1:-1, 1:-1].set(averaged)
    new_block = new_block.at[:, :, 1:-1, 0].add(correction[:, :, 0])
    new_block = new_block.at[:, :, 1:-1, -1].add(correction[:, :, 1])
    new_block = new_block.at[:, :, 0, 1:-1].add(correction[:, :, 2])
    new_block = new_block.at[:, :, -1, 1:-1].add(correction[:, :, 3])
    return new_block


def to_column(new_boxes):
    box_count = new_boxes.shape[0]
    return (
        new_boxes.reshape(box_count, NF, BZ, BXY, BXY)
        .transpose(1, 0, 2, 3, 4)
        .reshape(NF, box_count * BZ, BXY, BXY)
    )


def from_column(new_fields):
    box_count = new_fields.shape[1] // BZ
    return new_fields.reshape(NF, box_count, BZ * BXY * BXY).transpose(1, 0, 2)


def local(old_boxes, send_slot, arrival, coarse, coarse_flux):
    boxes_held = old_boxes[0, 0]
    send_table = send_slot[0, 0]
    arrive = arrival[0, 0]
    peers = send_table.shape[0]
    capacity = send_table.shape[1]
    box_shape = boxes_held.shape[1:]
    spare = jnp.concatenate([boxes_held, jnp.zeros((1,) + box_shape, boxes_held.dtype)], axis=0)
    outgoing = jnp.take(spare, send_table.reshape(-1), axis=0).reshape(
        (peers, capacity) + box_shape
    )
    arrived = lax.all_to_all(outgoing, "gy", split_axis=0, concat_axis=0, tiled=True)
    new_boxes = jnp.take(arrived.reshape((peers * capacity,) + box_shape), arrive, axis=0)
    fields = to_column(new_boxes)
    primitives = primitive(fields)
    padded = padded_2(fields, (("gy", 1),), 2)
    half_axis = lax.axis_size("gx") // 2
    edge = BXY // 2 + 2
    coarse_block = coarse[0, 0].reshape(NF, -1, edge, edge)
    coarse_faces = cycle_faces(coarse_block)
    ghosts_all = passed_along(expand(coarse_faces), "gx", half_axis)
    new_fields, side_flux = advance(fields, primitives, padded[:, :2], padded[:, -2:], ghosts_all)
    face_mean, averaged = restrict(new_fields, side_flux)
    layers = face_mean.shape[1]
    half_edge = BXY // 2
    outbound = jnp.concatenate(
        [
            face_mean.reshape(NF, layers, 4 * half_edge),
            averaged.reshape(NF, layers, half_edge * half_edge),
        ],
        axis=2,
    )
    returned = passed_along(outbound, "gx", half_axis)
    back_faces = returned[:, :, : 4 * half_edge].reshape(NF, layers, 4, half_edge)
    back_averaged = returned[:, :, 4 * half_edge :].reshape(NF, layers, half_edge, half_edge)
    register = coarse_flux[0, 0].reshape(NF, layers, 4, half_edge)
    new_block = coarse_update(coarse_block, back_faces, back_averaged, register)
    fine_boxes = from_column(new_fields)
    return (fine_boxes[None, None], new_block.reshape(1, 1, NF, -1))


def solution(mesh):
    return jax.shard_map(
        local,
        mesh=mesh,
        in_specs=(
            P("gx", "gy", None, None, None),
            P("gx", "gy", None, None),
            P("gx", "gy", None),
            P("gx", "gy", None, None),
            P("gx", "gy", None, None),
        ),
        out_specs=(P("gx", "gy", None, None, None), P("gx", "gy", None, None)),
        check_vma=False,
    )
```

profile of v0, /device:TPU:1, one launch (start us, length us, event | category | flops | bytes accessed | tf_op | source)
XLA Modules:
  0.0 110.1 jit_solution(2571092219173302896)
XLA Ops:
  0.6 0.8 reduce.23
  3.0 8.7 %collective-permute-start.2 = (f32[5,16,4,2,16]{4,1,3,2,0:T(8,128)S(1)}, f32[5,16,4,2,16]{4,1,3,2,0:T(8,128)S(1)}, u32[]{:S(2)}, u32[]{:S(2)}) collective-permute-start(f32[5,16,4,2,16]{4,1,3,2,0:T(8,128)S(1)} %broadcast_in_dim.37), channel_id=1, source_target_pairs={{0,512},{16,528},{32,544},{48,560},{64,576},{80,592},{96,608},{112... | collective-permute-start | bytes 122888 | tf_op jit(solution)/shard_map/ppermute | solution.py:31
  12.8 1.1 copy_select_fusion
  13.9 10.7 %all-to-all-start = ((f32[16,2,5,512]{3,1,2,0:T(2,128)}), f32[16,2,5,512]{3,1,2,0:T(2,128)S(1)}, u32[]{:S(2)}, u32[]{:S(2)}) async-start(f32[16,2,5,512]{3,1,2,0:T(2,128)} %copy_select_fusion), calls=%async_computation | async-start | bytes 655360 | tf_op jit(solution)/shard_map/all_to_all | solution.py:177
  25.9 11.7 %all-to-all-done = f32[16,2,5,512]{3,1,2,0:T(2,128)S(1)} async-done(((f32[16,2,5,512]{3,1,2,0:T(2,128)}), f32[16,2,5,512]{3,1,2,0:T(2,128)S(1)}, u32[]{:S(2)}, u32[]{:S(2)}) %all-to-all-start) | async-done | bytes 327712 | tf_op jit(solution)/shard_map/all_to_all | solution.py:177
  38.5 0.8 copy-done.2
  42.8 0.7 fusion.15
  46.0 0.9 copy-done.4
  48.6 1.0 fusion.47
  49.7 2.7 %copy.296 = f32[5,16,16,1]{0,2,1,3:T(8,128)S(1)} copy(f32[5,16,16,1]{3,2,1,0:T(8,128)} %get-tuple-element.198) | data formatting | bytes 10240 | tf_op jit(solution)/shard_map/slice | solution.py:128
  52.3 1.6 %copy.297 = f32[5,16,16,1]{0,2,1,3:T(8,128)S(1)} copy(f32[5,16,16,1]{3,2,1,0:T(8,128)S(1)} %get-tuple-element.199) | data formatting | bytes 10240 | tf_op jit(solution)/shard_map/slice | solution.py:128
  55.0 1.7 %collective-permute-start = (f32[5,2,16,16]{3,2,1,0:T(8,128)S(1)}, f32[5,2,16,16]{3,2,1,0:T(8,128)S(1)}, u32[]{:S(2)}, u32[]{:S(2)}) collective-permute-start(f32[5,2,16,16]{3,2,1,0:T(8,128)S(1)} %get-tuple-element.200), channel_id=1, source_target_pairs={{0,1},{1,2},{2,3},{3,4},{4,5},{5,6},{6,7},{7,8},{8,9},{9,10},{10,1... | collective-permute-start | bytes 30728 | tf_op jit(solution)/shard_map/ppermute | solution.py:22
  56.8 2.3 %collective-permute-done.1 = f32[5,2,16,16]{3,2,1,0:T(8,128)S(1)} collective-permute-done((f32[5,2,16,16]{3,2,1,0:T(8,128)S(1)}, f32[5,2,16,16]{3,2,1,0:T(8,128)S(1)}, u32[]{:S(2)}, u32[]{:S(2)}) %collective-permute-start.1) | collective-permute-done | bytes 10272 | tf_op jit(solution)/shard_map/ppermute | solution.py:23
  60.6 0.9 copy-done.5
  62.0 1.7 %copy.302 = f32[5,16,16,16]{0,3,2,1:T(8,128)S(1)} copy(f32[5,16,16,16]{3,2,1,0:T(8,128)S(1)} %fusion.14) | data formatting | bytes 163840 | tf_op jit(solution)/shard_map/sub | solution.py:126
  63.7 1.4 %reduce_sum.149 = f32[5,8,8,8]{0,3,2,1:T(8,128)S(1)} reduce(f32[5,8,2,8,2,8,2]{0,6,5,4,3,2,1:T(2,128)S(1)} %bitcast.153, f32[]{:T(128)} %constant.355.clone.1), dimensions={2,4,6}, to_apply=%region_11.12 | reduce | flops 17920 | bytes 92164 | tf_op jit(solution)/shard_map/reduce_sum | solution.py:137
  65.4 7.5 %collective-permute-start.3 = (f32[5,8,96]{2,1,0:T(8,128)S(1)}, f32[5,8,96]{2,1,0:T(8,128)S(1)}, u32[]{:S(2)}, u32[]{:S(2)}) collective-permute-start(f32[5,8,96]{2,1,0:T(8,128)S(1)} %pad_maximum_fusion.24), channel_id=1, source_target_pairs={{0,512},{16,528},{32,544},{48,560},{64,576},{80,592},{96,608},{112... | collective-permute-start | bytes 46088 | tf_op jit(solution)/shard_map/ppermute | solution.py:31
  73.7 1.0 reshape.576
  75.4 11.9 %scatter.4 = f32[5,8,10,10]{3,2,1,0:T(8,128)S(1)} dynamic-update-slice(f32[5,8,10,10]{3,2,1,0:T(8,128)S(1)} %reshape_squeeze.13, f32[5,8,8,8]{3,2,1,0:T(8,128)S(1)} %reshape.578, s32[]{:T(128)} %constant.350.clone.1, s32[]{:T(128)} %constant.350.clone.1, s32[]{:T(128)} %constant.362.clone.1, s32[]{:T(128)} %constant.362.clone.1) | dynamic-update-slice | bytes 20484 | tf_op jit(solution)/shard_map/scatter | solution.py:144
  88.4 6.0 %scatter-add.45 = f32[5,8,10,10]{3,2,1,0:T(8,128)S(1)} dynamic-update-slice(f32[5,8,10,10]{3,2,1,0:T(8,128)S(1)} %scatter-add.44, f32[5,8,8,1]{3,2,1,0:T(8,128)S(1)} %slice_add_fusion.2, s32[]{:T(128)} %constant.350.clone.1, s32[]{:T(128)} %constant.350.clone.1, s32[]{:T(128)} %constant.362.clone.1, s32[]{:T(128)} %constant.367.clone.1) | dynamic-update-slice | bytes 2564 | tf_op jit(solution)/shard_map/scatter-add | solution.py:146
  94.4 1.4 %slice_add_fusion.9 = f32[5,8,1,8]{3,2,1,0:T(1,128)S(1)} fusion(f32[5,8,4,8]{3,2,1,0:T(4,128)S(1)} %subtract_multiply_fusion, f32[5,8,10,10]{3,2,1,0:T(8,128)S(1)} %scatter-add.45, s32[]{:T(128)} %bitcast.66, s32[]{:T(128)} %bitcast.67), kind=kLoop, calls=%fused_computation.152 | loop fusion | flops 320 | bytes 3848 | tf_op jit(solution)/shard_map/add | solution.py:147
  95.8 7.4 %scatter-add.46 = f32[5,8,10,10]{3,2,1,0:T(8,128)S(1)} dynamic-update-slice(f32[5,8,10,10]{3,2,1,0:T(8,128)S(1)} %scatter-add.45, f32[5,8,1,8]{3,2,1,0:T(1,128)S(1)} %slice_add_fusion.9, s32[]{:T(128)} %constant.350.clone.1, s32[]{:T(128)} %constant.350.clone.1, s32[]{:T(128)} %bitcast.66, s32[]{:T(128)} %bitcast.67) | dynamic-update-slice | bytes 2564 | tf_op jit(solution)/shard_map/scatter-add | solution.py:147
  103.3 6.1 %scatter-add.49 = f32[5,8,10,10]{3,2,1,0:T(8,128)S(1)} dynamic-update-slice(f32[5,8,10,10]{3,2,1,0:T(8,128)S(1)} %scatter-add.46, f32[5,8,1,8]{3,2,1,0:T(1,128)S(1)} %slice_add_fusion.8, s32[]{:T(128)} %constant.350.clone.1, s32[]{:T(128)} %constant.350.clone.1, s32[]{:T(128)} %constant.367.clone.1, s32[]{:T(128)} %constant.362.clone.1) | dynamic-update-slice | bytes 2564 | tf_op jit(solution)/shard_map/scatter-add | solution.py:148
  109.4 0.8 reshape.601
  (149 shorter events, 17.9 us)
Async XLA Ops:
  0.6 11.1 %copy-start.12 = (s32[1,1,16,2]{2,3,1,0:T(2,128)S(1)}, s32[1,1,16,2]{2,3,1,0:T(2,128)}, u32[]{:S(2)}) copy-start(s32[1,1,16,2]{2,3,1,0:T(2,128)} %param.29) | copy-start | bytes 388
  0.6 11.2 %copy-start.10 = (f32[1,1,16,5,512]{4,2,3,1,0:T(8,128)S(1)}, f32[1,1,16,5,512]{4,2,3,1,0:T(8,128)}, u32[]{:S(2)}) copy-start(f32[1,1,16,5,512]{4,2,3,1,0:T(8,128)} %param.28) | copy-start | bytes 491524
  3.0 21.6 %copy-start.14 = (s32[1,1,8]{2,1,0:T(1,128)S(1)}, s32[1,1,8]{2,1,0:T(1,128)}, u32[]{:S(2)}) copy-start(s32[1,1,8]{2,1,0:T(1,128)} %param.30) | copy-start | bytes 100
  3.0 21.6 %collective-permute-start.2 = (f32[5,16,4,2,16]{4,1,3,2,0:T(8,128)S(1)}, f32[5,16,4,2,16]{4,1,3,2,0:T(8,128)S(1)}, u32[]{:S(2)}, u32[]{:S(2)}) collective-permute-start(f32[5,16,4,2,16]{4,1,3,2,0:T(8,128)S(1)} %broadcast_in_dim.37), channel_id=1, source_target_pairs={{0,512},{16,528},{32,544},{48,560},{64,576},{80,592},{96,608},{112... | collective-permute-start | bytes 122888 | tf_op jit(solution)/shard_map/ppermute | solution.py:31
  13.9 23.7 %all-to-all-start = ((f32[16,2,5,512]{3,1,2,0:T(2,128)}), f32[16,2,5,512]{3,1,2,0:T(2,128)S(1)}, u32[]{:S(2)}, u32[]{:S(2)}) async-start(f32[16,2,5,512]{3,1,2,0:T(2,128)} %copy_select_fusion), calls=%async_computation | async-start | bytes 655360 | tf_op jit(solution)/shard_map/all_to_all | solution.py:177
  25.8 15.5 %copy-start = (f32[5,16,1,2,16]{3,4,1,0,2:T(8,128)}, f32[5,16,1,2,16]{3,4,1,0,2:T(8,128)S(1)}, u32[]{:S(2)}) copy-start(f32[5,16,1,2,16]{3,4,1,0,2:T(8,128)S(1)} %copy.327) | copy-start | bytes 30724
  38.5 0.8 copy-start.2
  41.7 1.1 copy-start.1
  42.8 2.1 %copy-start.3 = (f32[8,5,2,16,16]{4,3,2,0,1:T(8,128)S(1)}, f32[8,5,2,16,16]{4,3,2,0,1:T(8,128)}, u32[]{:S(2)}) copy-start(f32[8,5,2,16,16]{4,3,2,0,1:T(8,128)} %copy-done.2) | copy-start | bytes 245764
  45.0 9.8 %copy-start.6 = (f32[8,5,2,16,16]{4,3,2,0,1:T(8,128)}, f32[8,5,2,16,16]{4,3,2,0,1:T(8,128)S(1)}, u32[]{:S(2)}) copy-start(f32[8,5,2,16,16]{4,3,2,0,1:T(8,128)S(1)} %broadcast_select_fusion) | copy-start | bytes 245764
  46.0 0.9 copy-start.4
  47.4 0.9 copy-start.8
  47.5 1.0 copy-start.9
  54.9 4.2 %collective-permute-start.1 = (f32[5,2,16,16]{3,2,1,0:T(8,128)S(1)}, f32[5,2,16,16]{3,2,1,0:T(8,128)S(1)}, u32[]{:S(2)}, u32[]{:S(2)}) collective-permute-start(f32[5,2,16,16]{3,2,1,0:T(8,128)S(1)} %get-tuple-element.201), channel_id=1, source_target_pairs={{1,0},{2,1},{3,2},{4,3},{5,4},{6,5},{7,6},{8,7},{9,8},{10,9},{11,1... | collective-permute-start | bytes 30728 | tf_op jit(solution)/shard_map/ppermute | solution.py:23
  55.0 4.0 %collective-permute-start = (f32[5,2,16,16]{3,2,1,0:T(8,128)S(1)}, f32[5,2,16,16]{3,2,1,0:T(8,128)S(1)}, u32[]{:S(2)}, u32[]{:S(2)}) collective-permute-start(f32[5,2,16,16]{3,2,1,0:T(8,128)S(1)} %get-tuple-element.200), channel_id=1, source_target_pairs={{0,1},{1,2},{2,3},{3,4},{4,5},{5,6},{6,7},{7,8},{8,9},{9,10},{10,1... | collective-permute-start | bytes 30728 | tf_op jit(solution)/shard_map/ppermute | solution.py:22
  60.2 1.2 %copy-start.5 = (f32[5,16,17,16]{3,2,1,0:T(8,128)S(1)}, f32[5,16,17,16]{3,2,1,0:T(8,128)}, u32[]{:S(2)}) copy-start(f32[5,16,17,16]{3,2,1,0:T(8,128)} %copy-done.4) | copy-start | bytes 261124
  60.3 1.4 %copy-start.7 = (f32[8,5,2,16,16]{4,3,2,0,1:T(8,128)S(1)}, f32[8,5,2,16,16]{4,3,2,0,1:T(8,128)}, u32[]{:S(2)}) copy-start(f32[8,5,2,16,16]{4,3,2,0,1:T(8,128)} %copy-done.6) | copy-start | bytes 245764
  63.7 9.8 %copy-start.11 = (f32[1,1,5,256]{3,1,2,0:T(1,128)S(1)}, f32[1,1,5,256]{3,1,2,0:T(1,128)}, u32[]{:S(2)}) copy-start(f32[1,1,5,256]{3,1,2,0:T(1,128)} %param.32) | copy-start | bytes 15364
  63.7 11.2 %copy-start.13 = (f32[4]{0:T(128)S(1)}, f32[4]{0:T(128)}, u32[]{:S(2)}) copy-start(f32[4]{0:T(128)} %constant.376) | copy-start | bytes 52
  65.4 9.3 %collective-permute-start.3 = (f32[5,8,96]{2,1,0:T(8,128)S(1)}, f32[5,8,96]{2,1,0:T(8,128)S(1)}, u32[]{:S(2)}, u32[]{:S(2)}) collective-permute-start(f32[5,8,96]{2,1,0:T(8,128)S(1)} %pad_maximum_fusion.24), channel_id=1, source_target_pairs={{0,512},{16,528},{32,544},{48,560},{64,576},{80,592},{96,608},{112... | collective-permute-start | bytes 46088 | tf_op jit(solution)/shard_map/ppermute | solution.py:31
where the time goes:
time: 111 us; the launch traced here: 110 us
  local copies, waits for them, and re-layouts  51.8 us (47%)
  starting transfers between devices  28.7 us (26%)
  other arithmetic  14.2 us (13%)
  waiting for transfers between devices  13.9 us (13%)
  between operations  1.51 us (1%)
    ppermute x2, starting transfers between devices, passed_along(): return lax.ppermute(value, axis, pairs)  16.3 us
    scatter x1, local copies, waits for them, and re-layouts, coarse_update(): new_block = coarse_block.at[:, :, 1:-1, 1:-1].set(averaged)  11.9 us
    all_to_all x1, waiting for transfers between devices, local(): lax.all_to_all(outgoing, 'gy', split_axis=0, concat_axis=0, tiled=True)  11.7 us
    all_to_all x1, starting transfers between devices, local(): lax.all_to_all(outgoing, 'gy', split_axis=0, concat_axis=0, tiled=True)  10.7 us
    scatter-add x1, local copies, waits for them, and re-layouts, coarse_update(): new_block = new_block.at[:, :, 0, 1:-1].add(correction[:, :, 2])  7.36 us
    scatter-add x1, local copies, waits for them, and re-layouts, coarse_update(): new_block = new_block.at[:, :, -1, 1:-1].add(correction[:, :, 3])  6.09 us
    scatter-add x1, local copies, waits for them, and re-layouts, coarse_update(): new_block = new_block.at[:, :, 1:-1, -1].add(correction[:, :, 1])  6 us
    unnamed x36, local copies, waits for them, and re-layouts  5.76 us
  transfers between devices with their start and end apart: 5, of which 2 were waited for; matrix products, arithmetic and copies ran while one was open for 5% of the time, Pallas kernels for 0%

commit v1 on v0

v1 whole, which is shorter than its diff:
```python
import jax
import jax.numpy as jnp
import numpy as np
from jax import lax
from jax.experimental import pallas as pl
from jax.experimental.pallas import tpu as pltpu
from jax.sharding import PartitionSpec as P

NF = 5
BXY = 16
EDGE = BXY // 2 + 2
CYCLE = EDGE * EDGE
LANES = 128
ROWS = 20
STEP_RATIO = 0.1
HIGHEST = lax.Precision.HIGHEST


def lane_iota():
    return lax.broadcasted_iota(jnp.int32, (8, LANES), 1)


def selection_matrices():
    ghost = np.zeros((LANES, 3 * LANES), np.float32)
    mean = np.zeros((5 * LANES, LANES), np.float32)
    for y in range(BXY):
        for x in range(BXY):
            lane = y * BXY + x
            cy, cx = (1 + y // 2, 1 + x // 2)
            mean[lane, cy * EDGE + cx] = 1.0 / 8.0
            if x == 0:
                ghost[cy * EDGE, lane] = 1.0
                mean[2 * LANES + lane, cy * EDGE] = -0.25
            if x == BXY - 1:
                ghost[cy * EDGE + EDGE - 1, lane] = 1.0
                mean[2 * LANES + lane, cy * EDGE + EDGE - 1] = 0.25
            if y == 0:
                ghost[cx, 2 * LANES + x] = 1.0
                mean[4 * LANES + x, cx] = -0.25
            if y == BXY - 1:
                ghost[(EDGE - 1) * EDGE + cx, 2 * LANES + LANES - BXY + x] = 1.0
                mean[4 * LANES + LANES - BXY + x, (EDGE - 1) * EDGE + cx] = 0.25
    register = np.zeros((LANES, LANES), np.float32)
    for t in range(BXY // 2):
        register[t, (1 + t) * EDGE] = 1.0
        register[8 + t, (1 + t) * EDGE + EDGE - 1] = -1.0
        register[16 + t, 1 + t] = 1.0
        register[24 + t, (EDGE - 1) * EDGE + 1 + t] = -1.0
    return (ghost, mean, register)


def minmod(a, b):
    return jnp.maximum(jnp.minimum(a, b), 0.0) + jnp.minimum(jnp.maximum(a, b), 0.0)


def primitive(u):
    inverse = 1.0 / u[0]
    v = [u[i] * inverse for i in (1, 2, 3)]
    pressure = 0.4 * (u[4] - 0.5 * u[0] * (v[0] * v[0] + v[1] * v[1] + v[2] * v[2]))
    return [u[0]] + v + [pressure]


def state_terms(q, normal):
    density, velocity, pressure = (q[0], q[1:4], q[4])
    kinetic = velocity[0] * velocity[0] + velocity[1] * velocity[1] + velocity[2] * velocity[2]
    energy = 2.5 * pressure + 0.5 * density * kinetic
    momentum = [density * v for v in velocity]
    vn = velocity[normal]
    mass = momentum[normal]
    flux = [mass] + [mass * v for v in velocity] + [(energy + pressure) * vn]
    flux[1 + normal] = flux[1 + normal] + pressure
    scaled = 1.4 * pressure
    speed = jnp.abs(vn) + scaled * lax.rsqrt(scaled * density)
    return ([density] + momentum + [energy], flux, speed)


def face_flux(lower, upper, normal):
    cons_l, flux_l, speed_l = state_terms(lower, normal)
    cons_u, flux_u, speed_u = state_terms(upper, normal)
    half = 0.5 * jnp.maximum(speed_l, speed_u)
    return [
        0.5 * (fl + fu) - half * (cu - cl) for fl, fu, cl, cu in zip(flux_l, flux_u, cons_l, cons_u)
    ]


def lane_roll(value, shift):
    return pltpu.roll(value, shift % LANES, 1)


def pack_kernel(slots_ref, boxes_ref, out_ref):
    def one(d, carry):
        first = slots_ref[0, d]

        @pl.when(first < boxes_ref.shape[1])
        def _():
            second = jnp.minimum(slots_ref[1, d], boxes_ref.shape[1] - 1)
            for c, slot in enumerate((first, second)):
                for f in range(NF):
                    box = boxes_ref[f, pl.ds(slot, 1), :]
                    for q in range(4):
                        out_ref[d, pl.ds(c * ROWS + f * 4 + q, 1), :] = box[:, q * LANES : (q + 1) * LANES]

        return carry

    lax.fori_loop(0, out_ref.shape[0], one, 0)


def ghost_kernel(coarse_ref, flux_ref, ghost_m_ref, register_m_ref, ghosts_ref, base_ref):
    lane = lane_iota()
    row = lax.broadcasted_iota(jnp.int32, (8, LANES), 0)
    on_block = lane < CYCLE
    cy, cx = (lane // EDGE, lane % EDGE)
    interior = (cy >= 1) & (cy <= EDGE - 2) & (cx >= 1) & (cx <= EDGE - 2)
    blocks = []
    registers = []
    for f in range(NF):
        tiles = [coarse_ref[f, :, pl.ds(t * LANES, LANES)] for t in range(6)]
        tiles.append(
            jnp.concatenate(
                [coarse_ref[f, :, pl.ds(6 * LANES, 8 * CYCLE - 6 * LANES)], jnp.zeros((1, 7 * LANES - 8 * CYCLE), jnp.float32)],
                axis=1,
            )
        )
        rows = []
        for l in range(8):
            start = l * CYCLE
            t, off = divmod(start, LANES)
            first = jnp.broadcast_to(tiles[t], (8, LANES))
            piece = lane_roll(first, -off)
            if off + CYCLE > LANES:
                second = lane_roll(jnp.broadcast_to(tiles[t + 1], (8, LANES)), -off)
                piece = jnp.where(lane < LANES - off, piece, second)
            rows.append(piece)
        block = rows[0]
        for l in range(1, 8):
            block = jnp.where(row == l, rows[l], block)
        blocks.append(block)
        reg = None
        for l in range(8):
            t, off = divmod(l * 32, LANES)
            piece = lane_roll(jnp.broadcast_to(flux_ref[f, :, pl.ds(t * LANES, LANES)], (8, LANES)), -off)
            reg = piece if reg is None else jnp.where(row == l, piece, reg)
        registers.append(reg)
    safe = [jnp.where(on_block, b, 1.0) for b in blocks]
    prims = jnp.concatenate(primitive(safe), axis=0)
    spread = jnp.dot(prims, ghost_m_ref[...], precision=HIGHEST, preferred_element_type=jnp.float32)
    placed = jnp.dot(
        jnp.concatenate(registers, axis=0), register_m_ref[...], precision=HIGHEST, preferred_element_type=jnp.float32
    )
    for f in range(NF):
        for t in range(3):
            ghosts_ref[f, t] = spread[f * 8 : f * 8 + 8, t * LANES : (t + 1) * LANES]
        kept = jnp.where(on_block & ~interior, blocks[f], 0.0)
        base_ref[f] = kept + (0.5 * STEP_RATIO) * placed[f * 8 : f * 8 + 8]


def side_kernel(arrive_ref, received_ref, ghosts_ref, base_ref, mean_ref, part_ref, prim_ref, coarse_ref, fields):
    def one(k, carry):
        start = arrive_ref[0, k] * ROWS
        for f in range(NF):
            for q in range(4):
                fields[f, q, pl.ds(k, 1), :] = received_ref[pl.ds(start + f * 4 + q, 1), :]
        return carry

    lax.fori_loop(0, 8, one, 0)
    lane = lane_iota()
    x = lane % BXY
    first_x, last_x = (x == 0, x == BXY - 1)
    low_y, high_y = (lane < BXY, lane >= LANES - BXY)
    cells = [[fields[f, q] for f in range(NF)] for q in range(4)]
    prims = [primitive(c) for c in cells]
    ghost = [[ghosts_ref[f, t] for f in range(NF)] for t in range(3)]
    change = []
    x_sides = [None, None]
    for q in range(4):
        h = q % 2
        g = ghost[h]
        lower, upper, top = ([], [], [])
        for f in range(NF):
            p = prims[q][f]
            below = jnp.where(first_x, g[f], lane_roll(p, 1))
            above = jnp.where(last_x, g[f], lane_roll(p, -1))
            half = 0.5 * minmod(p - below, above - p)
            high = p + half
            lower.append(jnp.where(first_x, g[f], lane_roll(high, 1)))
            upper.append(p - half)
            top.append((high, jnp.where(last_x, g[f], p)))
        low_flux = face_flux(lower, upper, 0)
        top_flux = face_flux([t[0] for t in top], [t[1] for t in top], 0)
        change.append(
            [jnp.where(last_x, t, lane_roll(l, -1)) - l for l, t in zip(low_flux, top_flux)]
        )
        side = [jnp.where(first_x, l, jnp.where(last_x, t, 0.0)) for l, t in zip(low_flux, top_flux)]
        x_sides[h] = side if x_sides[h] is None else [a + b for a, b in zip(x_sides[h], side)]
    y_sides = None
    for j in range(2):
        q0, q1 = (2 * j, 2 * j + 1)
        g = ghost[2]
        states = ([], [], [], [], [], [])
        for f in range(NF):
            p0, p1 = (prims[q0][f], prims[q1][f])
            up0, up1 = (lane_roll(p0, BXY), lane_roll(p1, BXY))
            down0, down1 = (lane_roll(p0, -BXY), lane_roll(p1, -BXY))
            below0, below1 = (jnp.where(low_y, g[f], up0), jnp.where(low_y, up0, up1))
            above0, above1 = (jnp.where(high_y, down1, down0), jnp.where(high_y, g[f], down1))
            half0 = 0.5 * minmod(p0 - below0, above0 - p0)
            half1 = 0.5 * minmod(p1 - below1, above1 - p1)
            high0, high1 = (p0 + half0, p1 + half1)
            roll0, roll1 = (lane_roll(high0, BXY), lane_roll(high1, BXY))
            for one_list, value in zip(
                states,
                (
                    jnp.where(low_y, g[f], roll0),
                    p0 - half0,
                    jnp.where(low_y, roll0, roll1),
                    p1 - half1,
                    high1,
                    jnp.where(high_y, g[f], p1),
                ),
            ):
                one_list.append(value)
        flux0 = face_flux(states[0], states[1], 1)
        flux1 = face_flux(states[2], states[3], 1)
        top = face_flux(states[4], states[5], 1)
        for f in range(NF):
            next0, next1 = (lane_roll(flux0[f], -BXY), lane_roll(flux1[f], -BXY))
            change[q0][f] = change[q0][f] + (jnp.where(high_y, next1, next0) - flux0[f])
            change[q1][f] = change[q1][f] + (jnp.where(high_y, top[f], next1) - flux1[f])
        side = [jnp.where(low_y, a, jnp.where(high_y, b, 0.0)) for a, b in zip(flux0, top)]
        y_sides = side if y_sides is None else [a + b for a, b in zip(y_sides, side)]
    parts = [[c - STEP_RATIO * d for c, d in zip(cells[q], change[q])] for q in range(4)]
    for f in range(NF):
        for q in range(4):
            part_ref[f, q] = parts[q][f]
            prim_ref[f, q] = prims[q][f]
    scale = 0.5 * STEP_RATIO
    stacked = jnp.concatenate(
        [
            jnp.concatenate([parts[0][f] + parts[2][f] for f in range(NF)], axis=0),
            jnp.concatenate([parts[1][f] + parts[3][f] for f in range(NF)], axis=0),
            jnp.concatenate([scale * x_sides[0][f] for f in range(NF)], axis=0),
            jnp.concatenate([scale * x_sides[1][f] for f in range(NF)], axis=0),
            jnp.concatenate([scale * y_sides[f] for f in range(NF)], axis=0),
        ],
        axis=1,
    )
    coarse = jnp.dot(stacked, mean_ref[...], precision=HIGHEST, preferred_element_type=jnp.float32)
    for f in range(NF):
        coarse_ref[f] = base_ref[f] + coarse[f * 8 : f * 8 + 8]


def column_kernel(before_ref, after_ref, part_ref, prim_ref, coarse_ref, mean_ref, fine_ref, out_ref):
    lane = lane_iota()
    row = lax.broadcasted_iota(jnp.int32, (8, LANES), 0)
    first, last = (row == 0, row == 7)

    def down(value, edge):
        return jnp.where(first, edge, pltpu.roll(value, 1, 0))

    def up(value, edge):
        return jnp.where(last, edge, pltpu.roll(value, 7, 0))

    before = [primitive([before_ref[f * 4 + q : f * 4 + q + 1, :] for f in range(NF)]) for q in range(4)]
    after = [primitive([after_ref[f * 4 + q : f * 4 + q + 1, :] for f in range(NF)]) for q in range(4)]
    sums = []
    for h in range(2):
        states = ([], [], [], [], [], [])
        for f in range(NF):
            p0, p1 = (prim_ref[f, h], prim_ref[f, 2 + h])
            b0, b1 = (before[h][f], before[2 + h][f])
            a0, a1 = (after[h][f], after[2 + h][f])
            step = p1 - p0
            half0 = 0.5 * minmod(p0 - down(p1, b1), step)
            half1 = 0.5 * minmod(step, up(p0, a0) - p1)
            half_b = 0.5 * minmod(b1 - b0, p0[0:1] - b1)
            half_a = 0.5 * minmod(a0 - p1[7:8], a1 - a0)
            high1 = p1 + half1
            for one_list, value in zip(
                states,
                (down(high1, b1 + half_b), p0 - half0, p0 + half0, p1 - half1, high1[7:8], a0 - half_a),
            ):
                one_list.append(value)
        flux0 = face_flux(states[0], states[1], 2)
        flux1 = face_flux(states[2], states[3], 2)
        top = face_flux(states[4], states[5], 2)
        total = []
        for f in range(NF):
            flux2 = up(flux0[f], top[f])
            fine_ref[f, :, pl.ds(h * LANES, LANES)] = part_ref[f, h] - STEP_RATIO * (flux1[f] - flux0[f])
            fine_ref[f, :, pl.ds((2 + h) * LANES, LANES)] = part_ref[f, 2 + h] - STEP_RATIO * (flux2 - flux1[f])
            total.append(-STEP_RATIO * (flux2 - flux0[f]))
        sums.append(jnp.concatenate(total, axis=0))
    moved = jnp.dot(
        jnp.concatenate(sums, axis=1), mean_ref[: 2 * LANES], precision=HIGHEST, preferred_element_type=jnp.float32
    )
    cell = row * LANES + lane
    for f in range(NF):
        value = coarse_ref[f] + moved[f * 8 : f * 8 + 8]
        turned = value
        for bit in (1, 2, 4):
            turned = jnp.where(row & bit != 0, lane_roll(turned, bit * CYCLE), turned)
        flat = jnp.zeros((8, LANES), jnp.float32)
        for s in range(3):
            shifted = turned if s == 0 else pltpu.roll(turned, 8 - s, 0)
            flat = jnp.where(cell // CYCLE == row + s, shifted, flat)
        for t in range(6):
            out_ref[f, :, pl.ds(t * LANES, LANES)] = flat[t : t + 1]
        out_ref[f, :, pl.ds(6 * LANES, 8 * CYCLE - 6 * LANES)] = flat[6:7, : 8 * CYCLE - 6 * LANES]


def call(kernel, outs, in_spaces, name, flops, scratch=()):
    single = not isinstance(outs, list)
    shapes = [jax.ShapeDtypeStruct(s, jnp.float32) for s in ([outs] if single else outs)]
    specs = [pl.BlockSpec(memory_space=pltpu.VMEM) for _ in shapes]
    return pl.pallas_call(
        kernel,
        out_shape=shapes[0] if single else shapes,
        in_specs=[pl.BlockSpec(memory_space=space) for space in in_spaces],
        out_specs=specs[0] if single else specs,
        scratch_shapes=list(scratch),
        cost_estimate=pl.CostEstimate(flops=flops, bytes_accessed=500_000, transcendentals=0),
        compiler_params=pltpu.CompilerParams(vmem_limit_bytes=16 * 1024 * 1024),
        name=name,
    )


def passed_along(value, axis, steps):
    count = lax.axis_size(axis)
    return lax.ppermute(value, axis, [(source, (source + steps) % count) for source in range(count)])


def local(old_boxes, send_slot, arrival, coarse, coarse_flux):
    V, S = (pltpu.VMEM, pltpu.SMEM)
    ghost_m, mean_m, register_m = (jnp.asarray(m) for m in selection_matrices())
    half_axis = lax.axis_size("gx") // 2
    peers = send_slot.shape[2]
    boxes = jnp.transpose(old_boxes[0, 0], (1, 0, 2))
    outgoing = call(pack_kernel, (peers, 2 * ROWS, LANES), [S, V], "pack", 1_000_000)(
        send_slot[0, 0].T, boxes
    )
    received = lax.all_to_all(outgoing, "gy", split_axis=0, concat_axis=0, tiled=True)
    received = received.reshape(peers * 2 * ROWS, LANES)
    arrive = arrival[0]

    block = passed_along(jnp.transpose(coarse[0], (1, 0, 2)), "gx", half_axis)
    register = passed_along(jnp.transpose(coarse_flux[0], (1, 0, 2)), "gx", half_axis)
    ghosts, base = call(ghost_kernel, [(NF, 3, 8, LANES), (NF, 8, LANES)], [V] * 4, "ghosts", 10_000_000)(
        block, register, ghost_m, register_m
    )
    lowest = lax.dynamic_slice_in_dim(received, arrive[0, 0] * ROWS, ROWS, axis=0)
    highest = lax.dynamic_slice_in_dim(received, arrive[0, 7] * ROWS, ROWS, axis=0)
    before = passed_along(highest, "gy", 1)
    after = passed_along(lowest, "gy", -1)
    part, prim, summed = call(
        side_kernel,
        [(NF, 4, 8, LANES), (NF, 4, 8, LANES), (NF, 8, LANES)],
        [S, V, V, V, V],
        "sides",
        50_000_000,
        [pltpu.VMEM((NF, 4, 8, LANES), jnp.float32)],
    )(arrive, received, ghosts, base, mean_m)
    fine, block_new = call(
        column_kernel, [(NF, 8, 4 * LANES), (NF, 1, 8 * CYCLE)], [V] * 6, "column", 20_000_000
    )(before, after, part, prim, summed, mean_m)
    back = passed_along(block_new, "gx", half_axis)
    return (jnp.transpose(fine, (1, 0, 2))[None, None], jnp.transpose(back, (1, 0, 2))[None])


def solution(mesh):
    return jax.shard_map(
        local,
        mesh=mesh,
        in_specs=(
            P("gx", "gy", None, None, None),
            P("gx", "gy", None, None),
            P("gx", "gy", None),
            P("gx", "gy", None, None),
            P("gx", "gy", None, None),
        ),
        out_specs=(P("gx", "gy", None, None, None), P("gx", "gy", None, None)),
        check_vma=False,
    )
```

time: 111 us -> 49.8 us (0.45)
  the two profiles are of different devices: /device:TPU:1 before, /device:TPU:7 now
where the time goes in v1:
time: 49.8 us; the launch traced here: 49.5 us
  starting transfers between devices  31.3 us (63%)
  waiting for transfers between devices  9.05 us (18%)
  Pallas kernels  4.17 us (8%)
  local copies, waits for them, and re-layouts  2.82 us (6%)
  between operations  2.07 us (4%)
    all_to_all x1, starting transfers between devices, local(): lax.all_to_all(outgoing, 'gy', split_axis=0, concat_axis=0, tiled=True)  16.9 us
    ppermute x5, starting transfers between devices, passed_along(): lax.ppermute(value, axis, [(source, (source + steps) % count) for source...  14.5 us
    ppermute x5, waiting for transfers between devices, passed_along(): lax.ppermute(value, axis, [(source, (source + steps) % count) for source...  9.05 us
    unnamed x17, local copies, waits for them, and re-layouts  2.22 us
    pallas_call x1, Pallas kernels, local(): call(pack_kernel, (peers, 2 * ROWS, LANES), [S, V], 'pack', 1000000)  1.62 us
    pallas_call x1, Pallas kernels, local(): call(side_kernel, [(NF, 4, 8, LANES), (NF, 4, 8, LANES), (NF, 8, LANES)],...  1.31 us
  transfers between devices with their start and end apart: 6, of which 2 were waited for; matrix products, arithmetic and copies ran while one was open for 1% of the time, Pallas kernels for 3%

profile of v1, /device:TPU:7, one launch (start us, length us, event | category | flops | bytes accessed | tf_op | source)
XLA Modules:
  0.0 49.5 jit_solution(4856195892930344997)
XLA Ops:
  0.6 0.0 copy-start.5
  0.6 0.7 %copy-done.5 = s32[1,1,16,2]{2,3,1,0:T(2,128)S(1)} copy-done((s32[1,1,16,2]{2,3,1,0:T(2,128)S(1)}, s32[1,1,16,2]{2,3,1,0:T(2,128)}, u32[]{:S(2)}) %copy-start.5) | copy-done | bytes 152
  1.3 0.9 %copy-done.2 = f32[1,1,16,5,512]{4,2,3,1,0:T(8,128)S(1)} copy-done((f32[1,1,16,5,512]{4,2,3,1,0:T(8,128)S(1)}, f32[1,1,16,5,512]{4,2,3,1,0:T(8,128)}, u32[]{:S(2)}) %copy-start.2) | copy-done | bytes 163864
  2.2 1.6 %pack.1 = f32[16,40,128]{2,1,0:T(8,128)} custom-call(s32[2,16]{1,0:T(2,128)S(1)} %bitcast.23, f32[5,16,512]{2,1,0:T(8,128)S(1)} %bitcast.20), custom_call_target="tpu_custom_call" | custom-call | flops 1000000 | bytes 500000 | tf_op jit(solution)/shard_map/pack/pallas_call | solution.py:338
  3.9 0.0 copy-start.3
  3.9 16.9 %all-to-all-start = ((f32[16,40,128]{2,1,0:T(8,128)}), f32[16,40,128]{2,1,0:T(8,128)S(1)}, u32[]{:S(2)}, u32[]{:S(2)}) async-start(f32[16,40,128]{2,1,0:T(8,128)} %pack.1), calls=%async_computation | async-start | bytes 655360 | tf_op jit(solution)/shard_map/all_to_all | solution.py:341
  20.8 0.0 copy-done.6
  20.8 2.1 %collective-permute-start.2 = (f32[5,1,800]{2,1,0:T(1,128)S(1)}, f32[5,1,800]{2,1,0:T(1,128)S(1)}, u32[]{:S(2)}, u32[]{:S(2)}) collective-permute-start(f32[5,1,800]{2,1,0:T(1,128)S(1)} %bitcast.26), channel_id=1, source_target_pairs={{0,512},{16,528},{32,544},{48,560},{64,576},{80,592},{96,608},{112... | collective-permute-start | bytes 48008 | tf_op jit(solution)/shard_map/ppermute | solution.py:329
  22.8 0.0 copy-done.7
  22.8 7.3 %collective-permute-start.3 = (f32[5,1,256]{2,1,0:T(1,128)S(1)}, f32[5,1,256]{2,1,0:T(1,128)S(1)}, u32[]{:S(2)}, u32[]{:S(2)}) collective-permute-start(f32[5,1,256]{2,1,0:T(1,128)S(1)} %bitcast.27), channel_id=1, source_target_pairs={{0,512},{16,528},{32,544},{48,560},{64,576},{80,592},{96,608},{112... | collective-permute-start | bytes 15368 | tf_op jit(solution)/shard_map/ppermute | solution.py:329
  30.1 0.6 %fusion = (s32[1,1]{1,0:T(1,128)}, s32[1,1]{1,0:T(1,128)}) fusion(s32[1,8]{1,0:T(1,128)S(1)} %bitcast.21), kind=kLoop, calls=%fused_computation.2 | loop fusion | bytes 16 | tf_op jit(solution)/shard_map/slice | solution.py:350
  32.0 0.0 all-to-all-done
  32.1 3.2 %collective-permute-start = (f32[20,128]{1,0:T(8,128)S(1)}, f32[20,128]{1,0:T(8,128)S(1)}, u32[]{:S(2)}, u32[]{:S(2)}) collective-permute-start(f32[20,128]{1,0:T(8,128)S(1)} %get-tuple-element.19), channel_id=1, source_target_pairs={{0,1},{1,2},{2,3},{3,4},{4,5},{5,6},{6,7},{7,8},{8,9},{9,10},{10,1... | collective-permute-start | bytes 30728 | tf_op jit(solution)/shard_map/ppermute | solution.py:329
  35.3 0.0 collective-permute-start.1
  35.3 0.0 collective-permute-done.3.flux_ref
  35.3 0.0 collective-permute-done.2.coarse_ref
  35.3 0.4 ghosts.1
  35.7 1.3 %sides.1 = (f32[5,4,8,128]{3,2,1,0:T(8,128)S(1)}, f32[5,4,8,128]{3,2,1,0:T(8,128)S(1)}, f32[5,8,128]{2,1,0:T(8,128)S(1)}) custom-call(s32[1,8]{1,0:T(1,128)S(1)} %bitcast.22, f32[640,128]{1,0:T(8,128)S(1)} %bitcast.19, f32[5,3,8,128]{3,2,1,0:T(8,128)S(1)} %get-tuple-element.9.ghosts_ref, f32[5,8,128]{2,1,0:T(8,128)S(1)} %get-tuple-element.10.base_ref, ...), custom_call_target="tpu_custom_call" | custom-call | flops 50000000 | bytes 500000 | tf_op jit(solution)/shard_map/sides/pallas_call | solution.py:354
  37.0 0.0 collective-permute-done.before_ref
  37.0 2.6 %collective-permute-done.1.after_ref = f32[20,128]{1,0:T(8,128)S(1)} collective-permute-done((f32[20,128]{1,0:T(8,128)S(1)}, f32[20,128]{1,0:T(8,128)S(1)}, u32[]{:S(2)}, u32[]{:S(2)}) %collective-permute-start.1) | collective-permute-done | bytes 10272 | tf_op jit(solution)/shard_map/ppermute | solution.py:329
  39.6 0.8 %column.1 = (f32[5,8,512]{2,1,0:T(8,128)}, f32[5,1,800]{2,1,0:T(1,128)S(1)}) custom-call(f32[20,128]{1,0:T(8,128)S(1)} %collective-permute-done.before_ref, f32[20,128]{1,0:T(8,128)S(1)} %collective-permute-done.1.after_ref, f32[5,4,8,128]{3,2,1,0:T(8,128)S(1)} %get-tuple-element.11.part_ref, f32[5,4,8,128]{3,2,1,0:T(8,128)S(1)} %get-tuple-element.12.prim_ref, ...), custom_call_target="tpu_custom_call" | custom-call | flops 20000000 | bytes 500000 | tf_op jit(solution)/shard_map/column/pallas_call | solution.py:362
  40.5 1.9 %collective-permute-start.4 = (f32[5,1,800]{2,1,0:T(1,128)S(1)}, f32[5,1,800]{2,1,0:T(1,128)S(1)}, u32[]{:S(2)}, u32[]{:S(2)}) collective-permute-start(f32[5,1,800]{2,1,0:T(1,128)S(1)} %get-tuple-element.15), channel_id=1, source_target_pairs={{0,512},{16,528},{32,544},{48,560},{64,576},{80,592},{96,608},{112... | collective-permute-start | bytes 48008 | tf_op jit(solution)/shard_map/ppermute | solution.py:329
  42.4 6.5 %collective-permute-done.4 = f32[5,1,800]{2,1,0:T(1,128)S(1)} collective-permute-done((f32[5,1,800]{2,1,0:T(1,128)S(1)}, f32[5,1,800]{2,1,0:T(1,128)S(1)}, u32[]{:S(2)}, u32[]{:S(2)}) %collective-permute-start.4) | collective-permute-done | bytes 16032 | tf_op jit(solution)/shard_map/ppermute | solution.py:329
  48.8 0.6 %copy.12 = f32[1,1,5,800]{3,1,2,0:T(1,128)} copy(f32[1,1,5,800]{3,1,2,0:T(1,128)S(1)} %bitcast.24) | data formatting | bytes 32000
  (11 shorter events, 0.0 us)
Async XLA Ops:
  0.6 0.7 %copy-start.5 = (s32[1,1,16,2]{2,3,1,0:T(2,128)S(1)}, s32[1,1,16,2]{2,3,1,0:T(2,128)}, u32[]{:S(2)}) copy-start(s32[1,1,16,2]{2,3,1,0:T(2,128)} %param.9) | copy-start | bytes 388
  1.3 0.9 %copy-start.2 = (f32[1,1,16,5,512]{4,2,3,1,0:T(8,128)S(1)}, f32[1,1,16,5,512]{4,2,3,1,0:T(8,128)}, u32[]{:S(2)}) copy-start(f32[1,1,16,5,512]{4,2,3,1,0:T(8,128)} %param.8) | copy-start | bytes 491524
  3.8 16.9 %copy-start.6 = (f32[1,1,5,800]{3,1,2,0:T(1,128)S(1)}, f32[1,1,5,800]{3,1,2,0:T(1,128)}, u32[]{:S(2)}) copy-start(f32[1,1,5,800]{3,1,2,0:T(1,128)} %param.11) | copy-start | bytes 48004
  3.8 19.0 %copy-start.7 = (f32[1,1,5,256]{3,1,2,0:T(1,128)S(1)}, f32[1,1,5,256]{3,1,2,0:T(1,128)}, u32[]{:S(2)}) copy-start(f32[1,1,5,256]{3,1,2,0:T(1,128)} %param.12) | copy-start | bytes 15364
  3.8 26.3 %copy-start.4 = (s32[1,1,8]{2,1,0:T(1,128)S(1)}, s32[1,1,8]{2,1,0:T(1,128)}, u32[]{:S(2)}) copy-start(s32[1,1,8]{2,1,0:T(1,128)} %param.10) | copy-start | bytes 100
  3.8 31.4 %copy-start.1 = (f32[128,384]{1,0:T(8,128)S(1)}, f32[128,384]{1,0:T(8,128)}, u32[]{:S(2)}) copy-start(f32[128,384]{1,0:T(8,128)} %constant.14.clone.ghost_m_ref) | copy-start | bytes 589828
  3.9 31.5 %copy-start.3 = (f32[128,128]{1,0:T(8,128)S(1)}, f32[128,128]{1,0:T(8,128)}, u32[]{:S(2)}) copy-start(f32[128,128]{1,0:T(8,128)} %constant.16.clone.register_m_ref) | copy-start | bytes 196612
  3.9 28.2 %all-to-all-start = ((f32[16,40,128]{2,1,0:T(8,128)}), f32[16,40,128]{2,1,0:T(8,128)S(1)}, u32[]{:S(2)}, u32[]{:S(2)}) async-start(f32[16,40,128]{2,1,0:T(8,128)} %pack.1), calls=%async_computation | async-start | bytes 655360 | tf_op jit(solution)/shard_map/all_to_all | solution.py:341
  20.8 15.0 %copy-start = (f32[640,128]{1,0:T(8,128)S(1)}, f32[640,128]{1,0:T(8,128)}, u32[]{:S(2)}) copy-start(f32[640,128]{1,0:T(8,128)} %constant.15.clone.mean_ref) | copy-start | bytes 983044
  20.8 14.5 %collective-permute-start.2 = (f32[5,1,800]{2,1,0:T(1,128)S(1)}, f32[5,1,800]{2,1,0:T(1,128)S(1)}, u32[]{:S(2)}, u32[]{:S(2)}) collective-permute-start(f32[5,1,800]{2,1,0:T(1,128)S(1)} %bitcast.26), channel_id=1, source_target_pairs={{0,512},{16,528},{32,544},{48,560},{64,576},{80,592},{96,608},{112... | collective-permute-start | bytes 48008 | tf_op jit(solution)/shard_map/ppermute | solution.py:329
  22.8 12.4 %collective-permute-start.3 = (f32[5,1,256]{2,1,0:T(1,128)S(1)}, f32[5,1,256]{2,1,0:T(1,128)S(1)}, u32[]{:S(2)}, u32[]{:S(2)}) collective-permute-start(f32[5,1,256]{2,1,0:T(1,128)S(1)} %bitcast.27), channel_id=1, source_target_pairs={{0,512},{16,528},{32,544},{48,560},{64,576},{80,592},{96,608},{112... | collective-permute-start | bytes 15368 | tf_op jit(solution)/shard_map/ppermute | solution.py:329
  32.1 5.0 %collective-permute-start = (f32[20,128]{1,0:T(8,128)S(1)}, f32[20,128]{1,0:T(8,128)S(1)}, u32[]{:S(2)}, u32[]{:S(2)}) collective-permute-start(f32[20,128]{1,0:T(8,128)S(1)} %get-tuple-element.19), channel_id=1, source_target_pairs={{0,1},{1,2},{2,3},{3,4},{4,5},{5,6},{6,7},{7,8},{8,9},{9,10},{10,1... | collective-permute-start | bytes 30728 | tf_op jit(solution)/shard_map/ppermute | solution.py:329
  35.3 4.3 %collective-permute-start.1 = (f32[20,128]{1,0:T(8,128)S(1)}, f32[20,128]{1,0:T(8,128)S(1)}, u32[]{:S(2)}, u32[]{:S(2)}) collective-permute-start(f32[20,128]{1,0:T(8,128)S(1)} %get-tuple-element.18), channel_id=1, source_target_pairs={{0,15},{1,0},{2,1},{3,2},{4,3},{5,4},{6,5},{7,6},{8,7},{9,8},{10,9... | collective-permute-start | bytes 30728 | tf_op jit(solution)/shard_map/ppermute | solution.py:329
  40.5 8.4 %collective-permute-start.4 = (f32[5,1,800]{2,1,0:T(1,128)S(1)}, f32[5,1,800]{2,1,0:T(1,128)S(1)}, u32[]{:S(2)}, u32[]{:S(2)}) collective-permute-start(f32[5,1,800]{2,1,0:T(1,128)S(1)} %get-tuple-element.15), channel_id=1, source_target_pairs={{0,512},{16,528},{32,544},{48,560},{64,576},{80,592},{96,608},{112... | collective-permute-start | bytes 48008 | tf_op jit(solution)/shard_map/ppermute | solution.py:329

commit v2 on v1

--- a/solution.py
+++ b/solution.py
@@ -11,6 +11,8 @@
 EDGE = BXY // 2 + 2
 CYCLE = EDGE * EDGE
 LANES = 128
+STRIDE = 24
+FACES_AT = 896
 ROWS = 20
 STEP_RATIO = 0.1
 HIGHEST = lax.Precision.HIGHEST
@@ -87,25 +89,46 @@
     return pltpu.roll(value, shift % LANES, 1)
 
 
-def pack_kernel(slots_ref, boxes_ref, out_ref):
-    def one(d, carry):
+def pack_kernel(slots_hbm, boxes_hbm, coarse_hbm, flux_hbm, out_ref, sides_ref, slots_ref, boxes_ref, coarse_ref, flux_ref, sems):
+    cells, faces = (coarse_hbm.shape[2], flux_hbm.shape[2])
+    copies = [
+        pltpu.make_async_copy(slots_hbm, slots_ref, sems.at[0]),
+        pltpu.make_async_copy(boxes_hbm, boxes_ref, sems.at[1]),
+        pltpu.make_async_copy(coarse_hbm, coarse_ref, sems.at[2]),
+        pltpu.make_async_copy(flux_hbm, flux_ref, sems.at[3]),
+    ]
+    for one in copies:
+        one.start()
+    for one in copies:
+        one.wait()
+    for f in range(NF):
+        sides_ref[f, :, pl.ds(0, cells)] = coarse_ref[f]
+        sides_ref[f, :, pl.ds(FACES_AT, faces)] = flux_ref[f]
+    held = boxes_ref.shape[1]
+    row = lax.broadcasted_iota(jnp.int32, (8, LANES), 0)
+
+    def fill(d, carry):
         first = slots_ref[0, d]
 
-        @pl.when(first < boxes_ref.shape[1])
+        @pl.when(first < held)
         def _():
-            second = jnp.minimum(slots_ref[1, d], boxes_ref.shape[1] - 1)
-            for c, slot in enumerate((first, second)):
-                for f in range(NF):
-                    box = boxes_ref[f, pl.ds(slot, 1), :]
-                    for q in range(4):
-                        out_ref[d, pl.ds(c * ROWS + f * 4 + q, 1), :] = box[:, q * LANES : (q + 1) * LANES]
+            slots = (first, jnp.minimum(slots_ref[1, d], held - 1))
+            lines = [[boxes_ref[f, pl.ds(slot, 1), :] for f in range(NF)] for slot in slots]
+            for t in range(2 * ROWS // 8):
+                tile = None
+                for i in range(8):
+                    c, r = divmod(8 * t + i, ROWS)
+                    f, q = divmod(r, 4)
+                    line = jnp.broadcast_to(lines[c][f][:, q * LANES : (q + 1) * LANES], (8, LANES))
+                    tile = line if tile is None else jnp.where(row == i, line, tile)
+                out_ref[d, 8 * t : 8 * t + 8, :] = tile
 
         return carry
 
-    lax.fori_loop(0, out_ref.shape[0], one, 0)
-
-
-def ghost_kernel(coarse_ref, flux_ref, ghost_m_ref, register_m_ref, ghosts_ref, base_ref):
+    lax.fori_loop(0, out_ref.shape[0], fill, 0)
+
+
+def ghost_kernel(sides_ref, ghost_m_ref, register_m_ref, ghosts_ref, base_ref):
     lane = lane_iota()
     row = lax.broadcasted_iota(jnp.int32, (8, LANES), 0)
     on_block = lane < CYCLE
@@ -114,10 +137,10 @@
     blocks = []
     registers = []
     for f in range(NF):
-        tiles = [coarse_ref[f, :, pl.ds(t * LANES, LANES)] for t in range(6)]
+        tiles = [sides_ref[f, :, pl.ds(t * LANES, LANES)] for t in range(6)]
         tiles.append(
             jnp.concatenate(
-                [coarse_ref[f, :, pl.ds(6 * LANES, 8 * CYCLE - 6 * LANES)], jnp.zeros((1, 7 * LANES - 8 * CYCLE), jnp.float32)],
+                [sides_ref[f, :, pl.ds(6 * LANES, 8 * CYCLE - 6 * LANES)], jnp.zeros((1, 7 * LANES - 8 * CYCLE), jnp.float32)],
                 axis=1,
             )
         )
@@ -138,7 +161,7 @@
         reg = None
         for l in range(8):
             t, off = divmod(l * 32, LANES)
-            piece = lane_roll(jnp.broadcast_to(flux_ref[f, :, pl.ds(t * LANES, LANES)], (8, LANES)), -off)
+            piece = lane_roll(jnp.broadcast_to(sides_ref[f, :, pl.ds(FACES_AT + t * LANES, LANES)], (8, LANES)), -off)
             reg = piece if reg is None else jnp.where(row == l, piece, reg)
         registers.append(reg)
     safe = [jnp.where(on_block, b, 1.0) for b in blocks]
@@ -154,20 +177,16 @@
         base_ref[f] = kept + (0.5 * STEP_RATIO) * placed[f * 8 : f * 8 + 8]
 
 
-def side_kernel(arrive_ref, received_ref, ghosts_ref, base_ref, mean_ref, part_ref, prim_ref, coarse_ref, fields):
-    def one(k, carry):
-        start = arrive_ref[0, k] * ROWS
-        for f in range(NF):
-            for q in range(4):
-                fields[f, q, pl.ds(k, 1), :] = received_ref[pl.ds(start + f * 4 + q, 1), :]
-        return carry
-
-    lax.fori_loop(0, 8, one, 0)
+def side_kernel(arrive_ref, received_ref, ghosts_ref, base_ref, mean_ref, part_ref, prim_ref, coarse_ref, boxes):
+    for k in range(8):
+        source, c = (arrive_ref[0, k] // 2, arrive_ref[0, k] % 2)
+        box = jnp.where(c == 0, received_ref[source, :ROWS, :], received_ref[source, ROWS:, :])
+        boxes[k * STRIDE : k * STRIDE + ROWS, :] = box
     lane = lane_iota()
     x = lane % BXY
     first_x, last_x = (x == 0, x == BXY - 1)
     low_y, high_y = (lane < BXY, lane >= LANES - BXY)
-    cells = [[fields[f, q] for f in range(NF)] for q in range(4)]
+    cells = [[boxes[pl.ds(f * 4 + q, 8, stride=STRIDE), :] for f in range(NF)] for q in range(4)]
     prims = [primitive(c) for c in cells]
     ghost = [[ghosts_ref[f, t] for f in range(NF)] for t in range(3)]
     change = []
@@ -308,9 +327,9 @@
         out_ref[f, :, pl.ds(6 * LANES, 8 * CYCLE - 6 * LANES)] = flat[6:7, : 8 * CYCLE - 6 * LANES]
 
 
-def call(kernel, outs, in_spaces, name, flops, scratch=()):
+def call(kernel, outs, in_spaces, name, flops, scratch=(), vmem=16):
     single = not isinstance(outs, list)
-    shapes = [jax.ShapeDtypeStruct(s, jnp.float32) for s in ([outs] if single else outs)]
+    shapes = [s if isinstance(s, jax.ShapeDtypeStruct) else pltpu.VMEM(s, jnp.float32) for s in ([outs] if single else outs)]
     specs = [pl.BlockSpec(memory_space=pltpu.VMEM) for _ in shapes]
     return pl.pallas_call(
         kernel,
@@ -319,7 +338,7 @@
         out_specs=specs[0] if single else specs,
         scratch_shapes=list(scratch),
         cost_estimate=pl.CostEstimate(flops=flops, bytes_accessed=500_000, transcendentals=0),
-        compiler_params=pltpu.CompilerParams(vmem_limit_bytes=16 * 1024 * 1024),
+        compiler_params=pltpu.CompilerParams(vmem_limit_bytes=vmem * 1024 * 1024),
         name=name,
     )
 
@@ -330,22 +349,34 @@
 
 
 def local(old_boxes, send_slot, arrival, coarse, coarse_flux):
-    V, S = (pltpu.VMEM, pltpu.SMEM)
+    V, S, H = (pltpu.VMEM, pltpu.SMEM, pltpu.HBM)
     ghost_m, mean_m, register_m = (jnp.asarray(m) for m in selection_matrices())
     half_axis = lax.axis_size("gx") // 2
     peers = send_slot.shape[2]
     boxes = jnp.transpose(old_boxes[0, 0], (1, 0, 2))
-    outgoing = call(pack_kernel, (peers, 2 * ROWS, LANES), [S, V], "pack", 1_000_000)(
-        send_slot[0, 0].T, boxes
-    )
+    slots = send_slot[0, 0].T
+    block, register = (jnp.transpose(v[0], (1, 0, 2)) for v in (coarse, coarse_flux))
+    outgoing, sides = call(
+        pack_kernel,
+        [(peers, 2 * ROWS, LANES), (NF, 1, FACES_AT + register.shape[2])],
+        [H] * 4,
+        "pack",
+        1_000_000,
+        [
+            pltpu.SMEM(slots.shape, jnp.int32),
+            pltpu.VMEM(boxes.shape, jnp.float32),
+            pltpu.VMEM(block.shape, jnp.float32),
+            pltpu.VMEM(register.shape, jnp.float32),
+            pltpu.SemaphoreType.DMA((4,)),
+        ],
+    )(*(pltpu.with_memory_space_constraint(v, H) for v in (slots, boxes, block, register)))
     received = lax.all_to_all(outgoing, "gy", split_axis=0, concat_axis=0, tiled=True)
     received = received.reshape(peers * 2 * ROWS, LANES)
     arrive = arrival[0]
 
-    block = passed_along(jnp.transpose(coarse[0], (1, 0, 2)), "gx", half_axis)
-    register = passed_along(jnp.transpose(coarse_flux[0], (1, 0, 2)), "gx", half_axis)
-    ghosts, base = call(ghost_kernel, [(NF, 3, 8, LANES), (NF, 8, LANES)], [V] * 4, "ghosts", 10_000_000)(
-        block, register, ghost_m, register_m
+    sides = passed_along(sides, "gx", half_axis)
+    ghosts, base = call(ghost_kernel, [(NF, 3, 8, LANES), (NF, 8, LANES)], [V] * 3, "ghosts", 10_000_000)(
+        sides, ghost_m, register_m
     )
     lowest = lax.dynamic_slice_in_dim(received, arrive[0, 0] * ROWS, ROWS, axis=0)
     highest = lax.dynamic_slice_in_dim(received, arrive[0, 7] * ROWS, ROWS, axis=0)
@@ -357,13 +388,15 @@
         [S, V, V, V, V],
         "sides",
         50_000_000,
-        [pltpu.VMEM((NF, 4, 8, LANES), jnp.float32)],
-    )(arrive, received, ghosts, base, mean_m)
+        [pltpu.VMEM((8 * STRIDE, LANES), jnp.float32)],
+    )(arrive, received.reshape(peers, 2 * ROWS, LANES), ghosts, base, mean_m)
     fine, block_new = call(
-        column_kernel, [(NF, 8, 4 * LANES), (NF, 1, 8 * CYCLE)], [V] * 6, "column", 20_000_000
+        column_kernel, [jax.ShapeDtypeStruct((NF, 8, 4 * LANES), jnp.float32), (NF, 1, 8 * CYCLE)], [V] * 6, "column", 20_000_000
     )(before, after, part, prim, summed, mean_m)
-    back = passed_along(block_new, "gx", half_axis)
-    return (jnp.transpose(fine, (1, 0, 2))[None, None], jnp.transpose(back, (1, 0, 2))[None])
+    pairs = [[g, g + half_axis] for g in range(half_axis)]
+    both = lax.all_gather(jnp.transpose(block_new, (1, 0, 2))[None], "gx", axis_index_groups=pairs)
+    back = lax.dynamic_index_in_dim(both, jnp.where(lax.axis_index("gx") < half_axis, 1, 0), 0, keepdims=False)
+    return (jnp.transpose(fine, (1, 0, 2))[None, None], back)
 
 
 def solution(mesh):

time: 49.8 us -> 45.3 us (0.910)
  the two profiles are of different devices: /device:TPU:7 before, /device:TPU:1 now
where the time goes in v2:
time: 45.3 us; the launch traced here: 45.1 us
  starting transfers between devices  19.9 us (44%)
  waiting for transfers between devices  10.3 us (23%)
  blocking collectives  7.18 us (16%)
  Pallas kernels  4.49 us (10%)
  between operations  2.03 us (4%)
  local copies, waits for them, and re-layouts  1.23 us (3%)
    all_to_all x1, starting transfers between devices, local(): lax.all_to_all(outgoing, 'gy', split_axis=0, concat_axis=0, tiled=True)  17.3 us
    all_to_all x1, waiting for transfers between devices, local(): lax.all_to_all(outgoing, 'gy', split_axis=0, concat_axis=0, tiled=True)  9.07 us
    all_gather x1, blocking collectives, local(): lax.all_gather(jnp.transpose(block_new, (1, 0, 2))[None], 'gx', axis_inde...  7.18 us
    ppermute x3, starting transfers between devices, passed_along(): lax.ppermute(value, axis, [(source, (source + steps) % count) for source...  2.57 us
    pallas_call x1, Pallas kernels, local(): call(pack_kernel, [(peers, 2 * ROWS, LANES), (NF, 1, FACES_AT + register....  2.02 us
    pallas_call x1, Pallas kernels, local(): call(side_kernel, [(NF, 4, 8, LANES), (NF, 4, 8, LANES), (NF, 8, LANES)],...  1.24 us
    ppermute x3, waiting for transfers between devices, passed_along(): lax.ppermute(value, axis, [(source, (source + steps) % count) for source...  1.2 us
  transfers between devices with their start and end apart: 4, of which 2 were waited for; matrix products, arithmetic and copies ran while one was open for 1% of the time, Pallas kernels for 4%

profile of v2, /device:TPU:1, one launch (start us, length us, event | category | flops | bytes accessed | tf_op | source)
XLA Modules:
  0.0 45.1 jit_solution(4387647082103016146)
XLA Ops:
  0.6 2.0 %pack.1 = (f32[16,40,128]{2,1,0:T(8,128)}, f32[5,1,1152]{2,1,0:T(1,128)S(1)}) custom-call(s32[2,16]{1,0:T(2,128)} %bitcast.25, f32[5,16,512]{2,1,0:T(8,128)} %bitcast.21, f32[5,1,800]{2,1,0:T(1,128)} %bitcast.23, f32[5,1,256]{2,1,0:T(1,128)} %bitcast.24), custom_call_target="tpu_custom_call" | custom-call | flops 1000000 | bytes 500000 | tf_op jit(solution)/shard_map/pack/pallas_call | solution.py:359
  2.7 0.0 copy-start.3
  2.7 0.0 copy-start.1
  2.7 0.0 copy-start.2
  2.7 17.3 %all-to-all-start = ((f32[16,40,128]{2,1,0:T(8,128)}), f32[16,40,128]{2,1,0:T(8,128)S(1)}, u32[]{:S(2)}, u32[]{:S(2)}) async-start(f32[16,40,128]{2,1,0:T(8,128)} %get-tuple-element.11), calls=%async_computation | async-start | bytes 655360 | tf_op jit(solution)/shard_map/all_to_all | solution.py:373
  20.0 0.0 copy-start
  20.0 2.1 %collective-permute-start.2 = (f32[5,1,1152]{2,1,0:T(1,128)S(1)}, f32[5,1,1152]{2,1,0:T(1,128)S(1)}, u32[]{:S(2)}, u32[]{:S(2)}) collective-permute-start(f32[5,1,1152]{2,1,0:T(1,128)S(1)} %get-tuple-element.12), channel_id=1, source_target_pairs={{0,512},{16,528},{32,544},{48,560},{64,576},{80,592},{96,608},{112... | collective-permute-start | bytes 69128 | tf_op jit(solution)/shard_map/ppermute | solution.py:348
  22.1 0.0 copy-done.3
  22.1 0.6 %fusion = (s32[1,1]{1,0:T(1,128)}, s32[1,1]{1,0:T(1,128)}) fusion(s32[1,8]{1,0:T(1,128)S(1)} %bitcast.19), kind=kLoop, calls=%fused_computation.3 | loop fusion | bytes 16 | tf_op jit(solution)/shard_map/slice | solution.py:381
  24.0 9.1 %all-to-all-done.received_ref = f32[16,40,128]{2,1,0:T(8,128)S(1)} async-done(((f32[16,40,128]{2,1,0:T(8,128)}), f32[16,40,128]{2,1,0:T(8,128)S(1)}, u32[]{:S(2)}, u32[]{:S(2)}) %all-to-all-start) | async-done | bytes 327712 | tf_op jit(solution)/shard_map/all_to_all | solution.py:373
  33.0 0.0 collective-permute-start
  33.1 0.5 %collective-permute-start.1 = (f32[20,128]{1,0:T(8,128)S(1)}, f32[20,128]{1,0:T(8,128)S(1)}, u32[]{:S(2)}, u32[]{:S(2)}) collective-permute-start(f32[20,128]{1,0:T(8,128)S(1)} %get-tuple-element.20), channel_id=1, source_target_pairs={{0,15},{1,0},{2,1},{3,2},{4,3},{5,4},{6,5},{7,6},{8,7},{9,8},{10,9... | collective-permute-start | bytes 30728 | tf_op jit(solution)/shard_map/ppermute | solution.py:348
  33.6 0.0 collective-permute-done.2.sides_ref
  33.6 0.0 copy-done.1
  33.6 0.0 copy-done.2
  33.6 0.4 ghosts.1
  34.0 0.0 copy-done
  34.0 1.2 %sides.1 = (f32[5,4,8,128]{3,2,1,0:T(8,128)S(1)}, f32[5,4,8,128]{3,2,1,0:T(8,128)S(1)}, f32[5,8,128]{2,1,0:T(8,128)S(1)}) custom-call(s32[1,8]{1,0:T(1,128)S(1)} %bitcast.20, f32[16,40,128]{2,1,0:T(8,128)S(1)} %all-to-all-done.received_ref, f32[5,3,8,128]{3,2,1,0:T(8,128)S(1)} %get-tuple-element.13.ghosts_ref, f32[5,8,128]{2,1,0:T(8,128)S(1)} %get-tuple-element.14.base_ref, ...), custom_call_target="tpu_custom_call" | custom-call | flops 50000000 | bytes 500000 | tf_op jit(solution)/shard_map/sides/pallas_call | solution.py:385
  35.2 0.0 collective-permute-done.before_ref
  35.2 1.2 %collective-permute-done.1.after_ref = f32[20,128]{1,0:T(8,128)S(1)} collective-permute-done((f32[20,128]{1,0:T(8,128)S(1)}, f32[20,128]{1,0:T(8,128)S(1)}, u32[]{:S(2)}, u32[]{:S(2)}) %collective-permute-start.1) | collective-permute-done | bytes 10272 | tf_op jit(solution)/shard_map/ppermute | solution.py:348
  36.4 0.8 %column.1 = (f32[5,8,512]{2,1,0:T(8,128)}, f32[5,1,800]{2,1,0:T(1,128)S(1)}) custom-call(f32[20,128]{1,0:T(8,128)S(1)} %collective-permute-done.before_ref, f32[20,128]{1,0:T(8,128)S(1)} %collective-permute-done.1.after_ref, f32[5,4,8,128]{3,2,1,0:T(8,128)S(1)} %get-tuple-element.15.part_ref, f32[5,4,8,128]{3,2,1,0:T(8,128)S(1)} %get-tuple-element.16.prim_ref, ...), custom_call_target="tpu_custom_call" | custom-call | flops 20000000 | bytes 500000 | tf_op jit(solution)/shard_map/column/pallas_call | solution.py:393
  37.3 7.2 %all-gather = f32[10,1,800]{2,1,0:T(1,128)S(1)} all-gather(f32[5,1,800]{2,1,0:T(1,128)S(1)} %get-tuple-element.19), channel_id=2, replica_groups={{0,512},{16,528},{32,544},{48,560},{64,576},{80,592},{96,608},{112,624}..., dimensions={0}, use_global_device_ids=true | all-gather | bytes 48000 | tf_op jit(solution)/shard_map/all_gather | solution.py:397
  44.4 0.6 %dynamic-slice_bitcast_fusion = f32[1,1,5,800]{3,1,2,0:T(1,128)} fusion(f32[2,1,1,5,800]{4,1,3,2,0:T(1,128)S(1)} %bitcast.22, s32[]{:T(128)S(6)} %select_n.14), kind=kLoop, calls=%fused_computation | loop fusion | bytes 32004 | tf_op jit(solution)/shard_map/jit(dynamic_index_in_dim)/squeeze | solution.py:398
  (1 shorter events, 0.0 us)
Async XLA Ops:
  2.7 19.4 %copy-start.3 = (s32[1,1,8]{2,1,0:T(1,128)S(1)}, s32[1,1,8]{2,1,0:T(1,128)}, u32[]{:S(2)}) copy-start(s32[1,1,8]{2,1,0:T(1,128)} %param.10) | copy-start | bytes 100
  2.7 30.9 %copy-start.1 = (f32[128,384]{1,0:T(8,128)S(1)}, f32[128,384]{1,0:T(8,128)}, u32[]{:S(2)}) copy-start(f32[128,384]{1,0:T(8,128)} %constant.29.clone.ghost_m_ref) | copy-start | bytes 589828
  2.7 30.9 %copy-start.2 = (f32[128,128]{1,0:T(8,128)S(1)}, f32[128,128]{1,0:T(8,128)}, u32[]{:S(2)}) copy-start(f32[128,128]{1,0:T(8,128)} %constant.31.clone.register_m_ref) | copy-start | bytes 196612
  2.7 30.3 %all-to-all-start = ((f32[16,40,128]{2,1,0:T(8,128)}), f32[16,40,128]{2,1,0:T(8,128)S(1)}, u32[]{:S(2)}, u32[]{:S(2)}) async-start(f32[16,40,128]{2,1,0:T(8,128)} %get-tuple-element.11), calls=%async_computation | async-start | bytes 655360 | tf_op jit(solution)/shard_map/all_to_all | solution.py:373
  20.0 14.0 %copy-start = (f32[640,128]{1,0:T(8,128)S(1)}, f32[640,128]{1,0:T(8,128)}, u32[]{:S(2)}) copy-start(f32[640,128]{1,0:T(8,128)} %constant.30.clone.mean_ref) | copy-start | bytes 983044
  20.0 13.6 %collective-permute-start.2 = (f32[5,1,1152]{2,1,0:T(1,128)S(1)}, f32[5,1,1152]{2,1,0:T(1,128)S(1)}, u32[]{:S(2)}, u32[]{:S(2)}) collective-permute-start(f32[5,1,1152]{2,1,0:T(1,128)S(1)} %get-tuple-element.12), channel_id=1, source_target_pairs={{0,512},{16,528},{32,544},{48,560},{64,576},{80,592},{96,608},{112... | collective-permute-start | bytes 69128 | tf_op jit(solution)/shard_map/ppermute | solution.py:348
  33.0 2.2 %collective-permute-start = (f32[20,128]{1,0:T(8,128)S(1)}, f32[20,128]{1,0:T(8,128)S(1)}, u32[]{:S(2)}, u32[]{:S(2)}) collective-permute-start(f32[20,128]{1,0:T(8,128)S(1)} %get-tuple-element.21), channel_id=1, source_target_pairs={{0,1},{1,2},{2,3},{3,4},{4,5},{5,6},{6,7},{7,8},{8,9},{9,10},{10,1... | collective-permute-start | bytes 30728 | tf_op jit(solution)/shard_map/ppermute | solution.py:348
  33.1 3.4 %collective-permute-start.1 = (f32[20,128]{1,0:T(8,128)S(1)}, f32[20,128]{1,0:T(8,128)S(1)}, u32[]{:S(2)}, u32[]{:S(2)}) collective-permute-start(f32[20,128]{1,0:T(8,128)S(1)} %get-tuple-element.20), channel_id=1, source_target_pairs={{0,15},{1,0},{2,1},{3,2},{4,3},{5,4},{6,5},{7,6},{8,7},{9,8},{10,9... | collective-permute-start | bytes 30728 | tf_op jit(solution)/shard_map/ppermute | solution.py:348

commit v3 on v2

--- a/solution.py
+++ b/solution.py
@@ -1,3 +1,5 @@
+import functools
+
 import jax
 import jax.numpy as jnp
 import numpy as np
@@ -107,25 +109,17 @@
     held = boxes_ref.shape[1]
     row = lax.broadcasted_iota(jnp.int32, (8, LANES), 0)
 
-    def fill(d, carry):
-        first = slots_ref[0, d]
-
-        @pl.when(first < held)
-        def _():
-            slots = (first, jnp.minimum(slots_ref[1, d], held - 1))
-            lines = [[boxes_ref[f, pl.ds(slot, 1), :] for f in range(NF)] for slot in slots]
-            for t in range(2 * ROWS // 8):
-                tile = None
-                for i in range(8):
-                    c, r = divmod(8 * t + i, ROWS)
-                    f, q = divmod(r, 4)
-                    line = jnp.broadcast_to(lines[c][f][:, q * LANES : (q + 1) * LANES], (8, LANES))
-                    tile = line if tile is None else jnp.where(row == i, line, tile)
-                out_ref[d, 8 * t : 8 * t + 8, :] = tile
-
-        return carry
-
-    lax.fori_loop(0, out_ref.shape[0], fill, 0)
+    for d in range(out_ref.shape[0]):
+        slots = [jnp.minimum(slots_ref[c, d], held - 1) for c in range(2)]
+        lines = [[boxes_ref[f, pl.ds(slot, 1), :] for f in range(NF)] for slot in slots]
+        for t in range(2 * ROWS // 8):
+            tile = None
+            for i in range(8):
+                c, r = divmod(8 * t + i, ROWS)
+                f, q = divmod(r, 4)
+                line = jnp.broadcast_to(lines[c][f][:, q * LANES : (q + 1) * LANES], (8, LANES))
+                tile = line if tile is None else jnp.where(row == i, line, tile)
+            out_ref[d, 8 * t : 8 * t + 8, :] = tile
 
 
 def ghost_kernel(sides_ref, ghost_m_ref, register_m_ref, ghosts_ref, base_ref):
@@ -177,7 +171,7 @@
         base_ref[f] = kept + (0.5 * STEP_RATIO) * placed[f * 8 : f * 8 + 8]
 
 
-def side_kernel(arrive_ref, received_ref, ghosts_ref, base_ref, mean_ref, part_ref, prim_ref, coarse_ref, boxes):
+def side_kernel(arrive_ref, received_ref, ghosts_ref, base_ref, mean_ref, fine_ref, edge_ref, out_ref, boxes):
     for k in range(8):
         source, c = (arrive_ref[0, k] // 2, arrive_ref[0, k] % 2)
         box = jnp.where(c == 0, received_ref[source, :ROWS, :], received_ref[source, ROWS:, :])
@@ -247,11 +241,38 @@
             change[q1][f] = change[q1][f] + (jnp.where(high_y, top[f], next1) - flux1[f])
         side = [jnp.where(low_y, a, jnp.where(high_y, b, 0.0)) for a, b in zip(flux0, top)]
         y_sides = side if y_sides is None else [a + b for a, b in zip(y_sides, side)]
+    row = lax.broadcasted_iota(jnp.int32, (8, LANES), 0)
+    for h in range(2):
+        states = ([], [], [], [])
+        for f in range(NF):
+            p0, p1 = (prims[h][f], prims[2 + h][f])
+            step, under = (p1 - p0, pltpu.roll(p1, 1, 0))
+            half0 = 0.5 * minmod(p0 - under, step)
+            half1 = 0.5 * minmod(step, pltpu.roll(p0, 7, 0) - p1)
+            for one_list, value in zip(
+                states, (pltpu.roll(p1 + half1, 1, 0), p0 - half0, p0 + half0, p1 - half1)
+            ):
+                one_list.append(value)
+        flux0 = [jnp.where(row == 0, 0.0, v) for v in face_flux(states[0], states[1], 2)]
+        flux1 = [jnp.where((row == 0) | (row == 7), 0.0, v) for v in face_flux(states[2], states[3], 2)]
+        for f in range(NF):
+            change[h][f] = change[h][f] + (flux1[f] - flux0[f])
+            change[2 + h][f] = change[2 + h][f] + (pltpu.roll(flux0[f], 7, 0) - flux1[f])
     parts = [[c - STEP_RATIO * d for c, d in zip(cells[q], change[q])] for q in range(4)]
     for f in range(NF):
         for q in range(4):
-            part_ref[f, q] = parts[q][f]
-            prim_ref[f, q] = prims[q][f]
+            fine_ref[f, :, pl.ds(q * LANES, LANES)] = parts[q][f]
+        low, high = ([prims[h][f] for h in range(2)], [prims[2 + h][f] for h in range(2)])
+        bottom = {2: [v[0:1] for v in low], 3: [v[0:1] for v in high], 4: [v[1:2] for v in low]}
+        top = {0: [v[6:7] for v in high], 1: [v[7:8] for v in low], 2: [v[7:8] for v in high]}
+        for place in range(4):
+            for face in range(4):
+                have, cell = (bottom, place + face) if face < 2 else (top, place + face - 2)
+                if cell in have:
+                    for h in range(2):
+                        edge_ref[place, f, 2 * face + h : 2 * face + h + 1, :] = have[cell][h]
+                else:
+                    edge_ref[place, f, 2 * face : 2 * face + 2, :] = jnp.zeros((2, LANES), jnp.float32)
     scale = 0.5 * STEP_RATIO
     stacked = jnp.concatenate(
         [
@@ -264,81 +285,91 @@
         axis=1,
     )
     coarse = jnp.dot(stacked, mean_ref[...], precision=HIGHEST, preferred_element_type=jnp.float32)
-    for f in range(NF):
-        coarse_ref[f] = base_ref[f] + coarse[f * 8 : f * 8 + 8]
-
-
-def column_kernel(before_ref, after_ref, part_ref, prim_ref, coarse_ref, mean_ref, fine_ref, out_ref):
-    lane = lane_iota()
-    row = lax.broadcasted_iota(jnp.int32, (8, LANES), 0)
-    first, last = (row == 0, row == 7)
-
-    def down(value, edge):
-        return jnp.where(first, edge, pltpu.roll(value, 1, 0))
-
-    def up(value, edge):
-        return jnp.where(last, edge, pltpu.roll(value, 7, 0))
-
-    before = [primitive([before_ref[f * 4 + q : f * 4 + q + 1, :] for f in range(NF)]) for q in range(4)]
-    after = [primitive([after_ref[f * 4 + q : f * 4 + q + 1, :] for f in range(NF)]) for q in range(4)]
-    sums = []
-    for h in range(2):
-        states = ([], [], [], [], [], [])
-        for f in range(NF):
-            p0, p1 = (prim_ref[f, h], prim_ref[f, 2 + h])
-            b0, b1 = (before[h][f], before[2 + h][f])
-            a0, a1 = (after[h][f], after[2 + h][f])
-            step = p1 - p0
-            half0 = 0.5 * minmod(p0 - down(p1, b1), step)
-            half1 = 0.5 * minmod(step, up(p0, a0) - p1)
-            half_b = 0.5 * minmod(b1 - b0, p0[0:1] - b1)
-            half_a = 0.5 * minmod(a0 - p1[7:8], a1 - a0)
-            high1 = p1 + half1
-            for one_list, value in zip(
-                states,
-                (down(high1, b1 + half_b), p0 - half0, p0 + half0, p1 - half1, high1[7:8], a0 - half_a),
-            ):
-                one_list.append(value)
-        flux0 = face_flux(states[0], states[1], 2)
-        flux1 = face_flux(states[2], states[3], 2)
-        top = face_flux(states[4], states[5], 2)
-        total = []
-        for f in range(NF):
-            flux2 = up(flux0[f], top[f])
-            fine_ref[f, :, pl.ds(h * LANES, LANES)] = part_ref[f, h] - STEP_RATIO * (flux1[f] - flux0[f])
-            fine_ref[f, :, pl.ds((2 + h) * LANES, LANES)] = part_ref[f, 2 + h] - STEP_RATIO * (flux2 - flux1[f])
-            total.append(-STEP_RATIO * (flux2 - flux0[f]))
-        sums.append(jnp.concatenate(total, axis=0))
-    moved = jnp.dot(
-        jnp.concatenate(sums, axis=1), mean_ref[: 2 * LANES], precision=HIGHEST, preferred_element_type=jnp.float32
-    )
     cell = row * LANES + lane
     for f in range(NF):
-        value = coarse_ref[f] + moved[f * 8 : f * 8 + 8]
-        turned = value
+        value = base_ref[f] + coarse[f * 8 : f * 8 + 8]
         for bit in (1, 2, 4):
-            turned = jnp.where(row & bit != 0, lane_roll(turned, bit * CYCLE), turned)
+            value = jnp.where(row & bit != 0, lane_roll(value, bit * CYCLE), value)
         flat = jnp.zeros((8, LANES), jnp.float32)
-        for s in range(3):
-            shifted = turned if s == 0 else pltpu.roll(turned, 8 - s, 0)
-            flat = jnp.where(cell // CYCLE == row + s, shifted, flat)
+        for n in range(3):
+            shifted = value if n == 0 else pltpu.roll(value, 8 - n, 0)
+            flat = jnp.where(cell // CYCLE == row + n, shifted, flat)
         for t in range(6):
             out_ref[f, :, pl.ds(t * LANES, LANES)] = flat[t : t + 1]
         out_ref[f, :, pl.ds(6 * LANES, 8 * CYCLE - 6 * LANES)] = flat[6:7, : 8 * CYCLE - 6 * LANES]
 
 
-def call(kernel, outs, in_spaces, name, flops, scratch=(), vmem=16):
+def edge_kernel(before_ref, after_ref, edge_ref, mean_ref, fine_in, block_in, fine_ref, block_ref):
+    lane = lane_iota()
+    row = lax.broadcasted_iota(jnp.int32, (8, LANES), 0)
+    rims = primitive(
+        [
+            jnp.concatenate([before_ref[f * 4 : f * 4 + 4, :], after_ref[f * 4 : f * 4 + 4, :]], axis=0)
+            for f in range(NF)
+        ]
+    )
+    lower, upper = ([], [])
+    for f in range(NF):
+        under = jnp.where(row < 4, rims[f], edge_ref[0, f])
+        low = jnp.where(row < 2, pltpu.roll(rims[f], 6, 0), edge_ref[1, f])
+        high = jnp.where(row >= 6, pltpu.roll(rims[f], 2, 0), edge_ref[2, f])
+        over = jnp.where(row >= 4, rims[f], edge_ref[3, f])
+        step = high - low
+        lower.append(low + 0.5 * minmod(low - under, step))
+        upper.append(high - 0.5 * minmod(step, over - high))
+    flux = face_flux(lower, upper, 2)
+    stacked = jnp.concatenate(flux, axis=0)
+    means = [
+        jnp.dot(
+            stacked, mean_ref[h * LANES : (h + 1) * LANES], precision=HIGHEST, preferred_element_type=jnp.float32
+        )
+        for h in range(2)
+    ]
+    tail = 8 * CYCLE - 6 * LANES
+    for f in range(NF):
+        above = jnp.where(row < 2, pltpu.roll(flux[f], 6, 0), jnp.where(row < 4, 0.0, flux[f]))
+        below = jnp.where(row < 4, flux[f], jnp.where(row < 6, 0.0, pltpu.roll(flux[f], 2, 0)))
+        change = STEP_RATIO * (below - above)
+        for q in range(4):
+            at = pl.ds(q * LANES, LANES)
+            edges = jnp.where(row == 0, change[q : q + 1], jnp.where(row == 7, change[4 + q : 5 + q], 0.0))
+            fine_ref[f, :, at] = fine_in[f, :, at] + edges
+        first, last = ([m[f * 8 + r + h : f * 8 + r + h + 1] for h, m in enumerate(means)] for r in (0, 6))
+        block_ref[f, :, pl.ds(LANES, 4 * LANES)] = block_in[f, :, pl.ds(LANES, 4 * LANES)]
+        block_ref[f, :, pl.ds(0, LANES)] = block_in[f, :, pl.ds(0, LANES)] + STEP_RATIO * (first[0] + first[1])
+        turned = lane_roll(jnp.broadcast_to(STEP_RATIO * (last[0] + last[1]), (8, LANES)), 7 * CYCLE)
+        at = pl.ds(5 * LANES, LANES)
+        block_ref[f, :, at] = block_in[f, :, at] - jnp.where(lane >= 7 * CYCLE - 5 * LANES, turned, 0.0)[0:1]
+        at = pl.ds(6 * LANES, tail)
+        block_ref[f, :, at] = block_in[f, :, at] - turned[0:1, :tail]
+
+
+def store_kernel(half, fine_ref, both_ref, fine_hbm, block_hbm, sems):
+    partner = jnp.where(lax.axis_index("gx") < half, 1, 0)
+    copies = [
+        pltpu.make_async_copy(fine_ref, fine_hbm, sems.at[0]),
+        pltpu.make_async_copy(both_ref.at[partner], block_hbm, sems.at[1]),
+    ]
+    for one in copies:
+        one.start()
+    for one in copies:
+        one.wait()
+
+
+def call(kernel, outs, in_spaces, name, flops, scratch=()):
     single = not isinstance(outs, list)
     shapes = [s if isinstance(s, jax.ShapeDtypeStruct) else pltpu.VMEM(s, jnp.float32) for s in ([outs] if single else outs)]
-    specs = [pl.BlockSpec(memory_space=pltpu.VMEM) for _ in shapes]
+    specs = [
+        pl.BlockSpec(memory_space=pltpu.HBM if isinstance(s, jax.ShapeDtypeStruct) else pltpu.VMEM) for s in shapes
+    ]
     return pl.pallas_call(
         kernel,
         out_shape=shapes[0] if single else shapes,
         in_specs=[pl.BlockSpec(memory_space=space) for space in in_spaces],
         out_specs=specs[0] if single else specs,
         scratch_shapes=list(scratch),
-        cost_estimate=pl.CostEstimate(flops=flops, bytes_accessed=500_000, transcendentals=0),
-        compiler_params=pltpu.CompilerParams(vmem_limit_bytes=vmem * 1024 * 1024),
+        cost_estimate=pl.CostEstimate(flops=flops, bytes_accessed=flops // 100, transcendentals=0),
+        compiler_params=pltpu.CompilerParams(vmem_limit_bytes=16 * 1024 * 1024),
         name=name,
     )
 
@@ -375,28 +406,36 @@
     arrive = arrival[0]
 
     sides = passed_along(sides, "gx", half_axis)
-    ghosts, base = call(ghost_kernel, [(NF, 3, 8, LANES), (NF, 8, LANES)], [V] * 3, "ghosts", 10_000_000)(
+    ghosts, base = call(ghost_kernel, [(NF, 3, 8, LANES), (NF, 8, LANES)], [V] * 3, "ghosts", 0)(
         sides, ghost_m, register_m
     )
     lowest = lax.dynamic_slice_in_dim(received, arrive[0, 0] * ROWS, ROWS, axis=0)
     highest = lax.dynamic_slice_in_dim(received, arrive[0, 7] * ROWS, ROWS, axis=0)
     before = passed_along(highest, "gy", 1)
     after = passed_along(lowest, "gy", -1)
-    part, prim, summed = call(
+    fine_shape, block_shape = ((NF, 8, 4 * LANES), (NF, 1, 8 * CYCLE))
+    fine, edge, block_new = call(
         side_kernel,
-        [(NF, 4, 8, LANES), (NF, 4, 8, LANES), (NF, 8, LANES)],
+        [fine_shape, (4, NF, 8, LANES), block_shape],
         [S, V, V, V, V],
         "sides",
-        50_000_000,
+        2_000_000_000,
         [pltpu.VMEM((8 * STRIDE, LANES), jnp.float32)],
     )(arrive, received.reshape(peers, 2 * ROWS, LANES), ghosts, base, mean_m)
     fine, block_new = call(
-        column_kernel, [jax.ShapeDtypeStruct((NF, 8, 4 * LANES), jnp.float32), (NF, 1, 8 * CYCLE)], [V] * 6, "column", 20_000_000
-    )(before, after, part, prim, summed, mean_m)
+        edge_kernel, [fine_shape, block_shape], [V] * 6, "edges", 20_000_000
+    )(before, after, edge, mean_m, fine, block_new)
     pairs = [[g, g + half_axis] for g in range(half_axis)]
-    both = lax.all_gather(jnp.transpose(block_new, (1, 0, 2))[None], "gx", axis_index_groups=pairs)
-    back = lax.dynamic_index_in_dim(both, jnp.where(lax.axis_index("gx") < half_axis, 1, 0), 0, keepdims=False)
-    return (jnp.transpose(fine, (1, 0, 2))[None, None], back)
+    both = lax.all_gather(block_new, "gx", axis_index_groups=pairs)
+    fine, back = call(
+        functools.partial(store_kernel, half_axis),
+        [jax.ShapeDtypeStruct(v, jnp.float32) for v in (fine_shape, block_shape)],
+        [V, V],
+        "store",
+        1_000_000,
+        [pltpu.SemaphoreType.DMA((2,))],
+    )(fine, pltpu.with_memory_space_constraint(both, V))
+    return (jnp.transpose(fine, (1, 0, 2))[None, None], jnp.transpose(back, (1, 0, 2))[None])
 
 
 def solution(mesh):

time: 45.3 us -> 45.2 us (level)
  local copies, waits for them, and re-layouts: 1.23 us -> 0.62 us
    all_to_all x1, waiting for transfers between devices: 9.07 us -> 3.74 us  [local(): lax.all_to_all(outgoing, 'gy', split_axis=0, concat_axis=0, tiled=True)]
    ppermute x3, waiting for transfers between devices: 1.2 us -> 6.23 us  [passed_along(): lax.ppermute(value, axis, [(source, (source + steps) % count) for source...]
    squeeze x1 -> x0, local copies, waits for them, and re-layouts: 0.61 us -> none  [local(): lax.dynamic_index_in_dim(both, jnp.where(lax.axis_index('gx') < half_axis...]
    pallas_call x2 -> x3, Pallas kernels: 2.08 us -> 2.57 us  [the longest x1 1.55 us: local(): call(side_kernel, [fine_shape, (4, NF, 8, LANES), block_shape], [S, V, V,...]
  transfers between devices with their start and end apart: 4 -> 4, of which waited for: 2 -> 3; matrix products, arithmetic and copies ran while one was open for 1% -> 1% of each run, Pallas kernels for 4% -> 4%
where the time goes in v3:
time: 45.2 us; the launch traced here: 44.8 us
  starting transfers between devices  20.2 us (45%)
  waiting for transfers between devices  9.97 us (22%)
  blocking collectives  7.19 us (16%)
  Pallas kernels  4.8 us (11%)
  between operations  2.03 us (4%)
  local copies, waits for them, and re-layouts  0.62 us (1%)
    all_to_all x1, starting transfers between devices, local(): lax.all_to_all(outgoing, 'gy', split_axis=0, concat_axis=0, tiled=True)  17.6 us
    all_gather x1, blocking collectives, local(): both = lax.all_gather(block_new, 'gx', axis_index_groups=pairs)  7.19 us
    ppermute x3, waiting for transfers between devices, passed_along(): lax.ppermute(value, axis, [(source, (source + steps) % count) for source...  6.23 us
    all_to_all x1, waiting for transfers between devices, local(): lax.all_to_all(outgoing, 'gy', split_axis=0, concat_axis=0, tiled=True)  3.74 us
    ppermute x3, starting transfers between devices, passed_along(): lax.ppermute(value, axis, [(source, (source + steps) % count) for source...  2.57 us
    pallas_call x1, Pallas kernels, local(): call(pack_kernel, [(peers, 2 * ROWS, LANES), (NF, 1, FACES_AT + register....  1.84 us
    pallas_call x1, Pallas kernels, local(): call(side_kernel, [fine_shape, (4, NF, 8, LANES), block_shape], [S, V, V,...  1.55 us
  transfers between devices with their start and end apart: 4, of which 3 were waited for; matrix products, arithmetic and copies ran while one was open for 1% of the time, Pallas kernels for 4%

profile of v3, /device:TPU:1, one launch (start us, length us, event | category | flops | bytes accessed | tf_op | source)
XLA Modules:
  0.0 44.8 jit_solution(9251445446388915036)
XLA Ops:
  0.6 1.8 %pack.1 = (f32[16,40,128]{2,1,0:T(8,128)}, f32[5,1,1152]{2,1,0:T(1,128)S(1)}) custom-call(s32[2,16]{1,0:T(2,128)} %bitcast.26, f32[5,16,512]{2,1,0:T(8,128)} %bitcast.23, f32[5,1,800]{2,1,0:T(1,128)} %bitcast.24, f32[5,1,256]{2,1,0:T(1,128)} %bitcast.25), custom_call_target="tpu_custom_call" | custom-call | flops 1000000 | bytes 10000 | tf_op jit(solution)/shard_map/pack/pallas_call | solution.py:390
  2.5 0.0 copy-start.3
  2.5 0.0 copy-start.1
  2.5 0.0 copy-start.2
  2.5 17.6 %all-to-all-start = ((f32[16,40,128]{2,1,0:T(8,128)}), f32[16,40,128]{2,1,0:T(8,128)S(1)}, u32[]{:S(2)}, u32[]{:S(2)}) async-start(f32[16,40,128]{2,1,0:T(8,128)} %get-tuple-element.13), calls=%async_computation | async-start | bytes 655360 | tf_op jit(solution)/shard_map/all_to_all | solution.py:404
  20.1 0.0 copy-start
  20.1 2.1 %collective-permute-start.2 = (f32[5,1,1152]{2,1,0:T(1,128)S(1)}, f32[5,1,1152]{2,1,0:T(1,128)S(1)}, u32[]{:S(2)}, u32[]{:S(2)}) collective-permute-start(f32[5,1,1152]{2,1,0:T(1,128)S(1)} %get-tuple-element.14), channel_id=1, source_target_pairs={{0,512},{16,528},{32,544},{48,560},{64,576},{80,592},{96,608},{112... | collective-permute-start | bytes 69128 | tf_op jit(solution)/shard_map/ppermute | solution.py:379
  22.2 0.0 copy-done.3
  22.2 0.6 %fusion = (s32[1,1]{1,0:T(1,128)}, s32[1,1]{1,0:T(1,128)}) fusion(s32[1,8]{1,0:T(1,128)S(1)} %bitcast.21), kind=kLoop, calls=%fused_computation.2 | loop fusion | bytes 16 | tf_op jit(solution)/shard_map/slice | solution.py:412
  24.1 4.9 %collective-permute-done.2.sides_ref = f32[5,1,1152]{2,1,0:T(1,128)S(1)} collective-permute-done((f32[5,1,1152]{2,1,0:T(1,128)S(1)}, f32[5,1,1152]{2,1,0:T(1,128)S(1)}, u32[]{:S(2)}, u32[]{:S(2)}) %collective-permute-start.2) | collective-permute-done | bytes 23072 | tf_op jit(solution)/shard_map/ppermute | solution.py:379
  29.0 0.0 copy-done.1
  29.0 0.0 copy-done.2
  29.0 0.4 ghosts.1
  29.4 3.7 %all-to-all-done.received_ref = f32[16,40,128]{2,1,0:T(8,128)S(1)} async-done(((f32[16,40,128]{2,1,0:T(8,128)}), f32[16,40,128]{2,1,0:T(8,128)S(1)}, u32[]{:S(2)}, u32[]{:S(2)}) %all-to-all-start) | async-done | bytes 327712 | tf_op jit(solution)/shard_map/all_to_all | solution.py:404
  33.2 0.0 collective-permute-start
  33.2 0.5 %collective-permute-start.1 = (f32[20,128]{1,0:T(8,128)S(1)}, f32[20,128]{1,0:T(8,128)S(1)}, u32[]{:S(2)}, u32[]{:S(2)}) collective-permute-start(f32[20,128]{1,0:T(8,128)S(1)} %get-tuple-element.28), channel_id=1, source_target_pairs={{0,15},{1,0},{2,1},{3,2},{4,3},{5,4},{6,5},{7,6},{8,7},{9,8},{10,9... | collective-permute-start | bytes 30728 | tf_op jit(solution)/shard_map/ppermute | solution.py:379
  33.7 0.0 copy-done
  33.7 1.6 %sides.1 = (f32[5,8,512]{2,1,0:T(8,128)S(1)}, f32[4,5,8,128]{3,2,1,0:T(8,128)S(1)}, f32[5,1,800]{2,1,0:T(1,128)S(1)}) custom-call(s32[1,8]{1,0:T(1,128)S(1)} %bitcast.22, f32[16,40,128]{2,1,0:T(8,128)S(1)} %all-to-all-done.received_ref, f32[5,3,8,128]{3,2,1,0:T(8,128)S(1)} %get-tuple-element.15.ghosts_ref, f32[5,8,128]{2,1,0:T(8,128)S(1)} %get-tuple-element.16.base_ref, ...), custom_call_target="tpu_custom_call" | custom-call | flops 2000000000 | bytes 20000000 | tf_op jit(solution)/shard_map/sides/pallas_call | solution.py:417
  35.3 0.0 collective-permute-done.before_ref
  35.3 1.3 %collective-permute-done.1.after_ref = f32[20,128]{1,0:T(8,128)S(1)} collective-permute-done((f32[20,128]{1,0:T(8,128)S(1)}, f32[20,128]{1,0:T(8,128)S(1)}, u32[]{:S(2)}, u32[]{:S(2)}) %collective-permute-start.1) | collective-permute-done | bytes 10272 | tf_op jit(solution)/shard_map/ppermute | solution.py:379
  36.6 0.4 edges.1
  37.0 7.2 %all-gather = f32[10,1,800]{2,1,0:T(1,128)S(1)} all-gather(f32[5,1,800]{2,1,0:T(1,128)S(1)} %get-tuple-element.21), channel_id=2, replica_groups={{0,512},{16,528},{32,544},{48,560},{64,576},{80,592},{96,608},{112,624}..., dimensions={0}, use_global_device_ids=true | all-gather | bytes 48000 | tf_op jit(solution)/shard_map/all_gather | solution.py:429
  44.1 0.7 %store.1 = (f32[5,8,512]{2,1,0:T(8,128)}, f32[5,1,800]{2,1,0:T(1,128)}) custom-call(f32[5,8,512]{2,1,0:T(8,128)S(1)} %get-tuple-element.20.fine_ref, f32[2,5,1,800]{3,2,1,0:T(1,128)S(1)} %bitcast.20), custom_call_target="tpu_custom_call" | custom-call | flops 1000000 | bytes 10000 | tf_op jit(solution)/shard_map/store/pallas_call | solution.py:430
  (1 shorter events, 0.0 us)
Async XLA Ops:
  2.5 19.7 %copy-start.3 = (s32[1,1,8]{2,1,0:T(1,128)S(1)}, s32[1,1,8]{2,1,0:T(1,128)}, u32[]{:S(2)}) copy-start(s32[1,1,8]{2,1,0:T(1,128)} %param.10) | copy-start | bytes 100
  2.5 26.6 %copy-start.1 = (f32[128,384]{1,0:T(8,128)S(1)}, f32[128,384]{1,0:T(8,128)}, u32[]{:S(2)}) copy-start(f32[128,384]{1,0:T(8,128)} %constant.14.clone.ghost_m_ref) | copy-start | bytes 589828
  2.5 26.5 %copy-start.2 = (f32[128,128]{1,0:T(8,128)S(1)}, f32[128,128]{1,0:T(8,128)}, u32[]{:S(2)}) copy-start(f32[128,128]{1,0:T(8,128)} %constant.16.clone.register_m_ref) | copy-start | bytes 196612
  2.5 30.7 %all-to-all-start = ((f32[16,40,128]{2,1,0:T(8,128)}), f32[16,40,128]{2,1,0:T(8,128)S(1)}, u32[]{:S(2)}, u32[]{:S(2)}) async-start(f32[16,40,128]{2,1,0:T(8,128)} %get-tuple-element.13), calls=%async_computation | async-start | bytes 655360 | tf_op jit(solution)/shard_map/all_to_all | solution.py:404
  20.1 13.6 %copy-start = (f32[640,128]{1,0:T(8,128)S(1)}, f32[640,128]{1,0:T(8,128)}, u32[]{:S(2)}) copy-start(f32[640,128]{1,0:T(8,128)} %constant.15.clone.mean_ref) | copy-start | bytes 983044
  20.1 8.9 %collective-permute-start.2 = (f32[5,1,1152]{2,1,0:T(1,128)S(1)}, f32[5,1,1152]{2,1,0:T(1,128)S(1)}, u32[]{:S(2)}, u32[]{:S(2)}) collective-permute-start(f32[5,1,1152]{2,1,0:T(1,128)S(1)} %get-tuple-element.14), channel_id=1, source_target_pairs={{0,512},{16,528},{32,544},{48,560},{64,576},{80,592},{96,608},{112... | collective-permute-start | bytes 69128 | tf_op jit(solution)/shard_map/ppermute | solution.py:379
  33.2 2.1 %collective-permute-start = (f32[20,128]{1,0:T(8,128)S(1)}, f32[20,128]{1,0:T(8,128)S(1)}, u32[]{:S(2)}, u32[]{:S(2)}) collective-permute-start(f32[20,128]{1,0:T(8,128)S(1)} %get-tuple-element.29), channel_id=1, source_target_pairs={{0,1},{1,2},{2,3},{3,4},{4,5},{5,6},{6,7},{7,8},{8,9},{9,10},{10,1... | collective-permute-start | bytes 30728 | tf_op jit(solution)/shard_map/ppermute | solution.py:379
  33.2 3.4 %collective-permute-start.1 = (f32[20,128]{1,0:T(8,128)S(1)}, f32[20,128]{1,0:T(8,128)S(1)}, u32[]{:S(2)}, u32[]{:S(2)}) collective-permute-start(f32[20,128]{1,0:T(8,128)S(1)} %get-tuple-element.28), channel_id=1, source_target_pairs={{0,15},{1,0},{2,1},{3,2},{4,3},{5,4},{6,5},{7,6},{8,7},{9,8},{10,9... | collective-permute-start | bytes 30728 | tf_op jit(solution)/shard_map/ppermute | solution.py:379

commit v4 on v3

--- a/solution.py
+++ b/solution.py
@@ -368,7 +368,7 @@
         in_specs=[pl.BlockSpec(memory_space=space) for space in in_spaces],
         out_specs=specs[0] if single else specs,
         scratch_shapes=list(scratch),
-        cost_estimate=pl.CostEstimate(flops=flops, bytes_accessed=flops // 100, transcendentals=0),
+        cost_estimate=pl.CostEstimate(flops=flops, bytes_accessed=500_000, transcendentals=0),
         compiler_params=pltpu.CompilerParams(vmem_limit_bytes=16 * 1024 * 1024),
         name=name,
     )
@@ -406,7 +406,7 @@
     arrive = arrival[0]
 
     sides = passed_along(sides, "gx", half_axis)
-    ghosts, base = call(ghost_kernel, [(NF, 3, 8, LANES), (NF, 8, LANES)], [V] * 3, "ghosts", 0)(
+    ghosts, base = call(ghost_kernel, [(NF, 3, 8, LANES), (NF, 8, LANES)], [V] * 3, "ghosts", 10_000_000)(
         sides, ghost_m, register_m
     )
     lowest = lax.dynamic_slice_in_dim(received, arrive[0, 0] * ROWS, ROWS, axis=0)
@@ -419,7 +419,7 @@
         [fine_shape, (4, NF, 8, LANES), block_shape],
         [S, V, V, V, V],
         "sides",
-        2_000_000_000,
+        50_000_000,
         [pltpu.VMEM((8 * STRIDE, LANES), jnp.float32)],
     )(arrive, received.reshape(peers, 2 * ROWS, LANES), ghosts, base, mean_m)
     fine, block_new = call(

time: 45.2 us -> 45.1 us (level)
    ppermute x3, waiting for transfers between devices: 6.23 us -> 0.89 us  [passed_along(): lax.ppermute(value, axis, [(source, (source + steps) % count) for source...]
    all_to_all x1, waiting for transfers between devices: 3.74 us -> 9.07 us  [local(): lax.all_to_all(outgoing, 'gy', split_axis=0, concat_axis=0, tiled=True)]
  transfers between devices with their start and end apart: 4 -> 4, of which waited for: 3 -> 2; matrix products, arithmetic and copies ran while one was open for 1% -> 1% of each run, Pallas kernels for 4% -> 4%
where the time goes in v4:
time: 45.1 us; the launch traced here: 44.8 us
  starting transfers between devices  20.2 us (45%)
  waiting for transfers between devices  9.96 us (22%)
  blocking collectives  7.19 us (16%)
  Pallas kernels  4.8 us (11%)
  between operations  2.04 us (5%)
  local copies, waits for them, and re-layouts  0.62 us (1%)
    all_to_all x1, starting transfers between devices, local(): lax.all_to_all(outgoing, 'gy', split_axis=0, concat_axis=0, tiled=True)  17.6 us
    all_to_all x1, waiting for transfers between devices, local(): lax.all_to_all(outgoing, 'gy', split_axis=0, concat_axis=0, tiled=True)  9.07 us
    all_gather x1, blocking collectives, local(): both = lax.all_gather(block_new, 'gx', axis_index_groups=pairs)  7.19 us
    ppermute x3, starting transfers between devices, passed_along(): lax.ppermute(value, axis, [(source, (source + steps) % count) for source...  2.57 us
    pallas_call x1, Pallas kernels, local(): call(pack_kernel, [(peers, 2 * ROWS, LANES), (NF, 1, FACES_AT + register....  1.84 us
    pallas_call x1, Pallas kernels, local(): call(side_kernel, [fine_shape, (4, NF, 8, LANES), block_shape], [S, V, V,...  1.55 us
  transfers between devices with their start and end apart: 4, of which 2 were waited for; matrix products, arithmetic and copies ran while one was open for 1% of the time, Pallas kernels for 4%

profile of v4, /device:TPU:1, one launch (start us, length us, event | category | flops | bytes accessed | tf_op | source)
XLA Modules:
  0.0 44.8 jit_solution(3311774936058989706)
XLA Ops:
  0.6 1.8 %pack.1 = (f32[16,40,128]{2,1,0:T(8,128)}, f32[5,1,1152]{2,1,0:T(1,128)S(1)}) custom-call(s32[2,16]{1,0:T(2,128)} %bitcast.26, f32[5,16,512]{2,1,0:T(8,128)} %bitcast.23, f32[5,1,800]{2,1,0:T(1,128)} %bitcast.24, f32[5,1,256]{2,1,0:T(1,128)} %bitcast.25), custom_call_target="tpu_custom_call" | custom-call | flops 1000000 | bytes 500000 | tf_op jit(solution)/shard_map/pack/pallas_call | solution.py:390
  2.5 0.0 copy-start.3
  2.5 0.0 copy-start.1
  2.5 0.0 copy-start.2
  2.5 17.6 %all-to-all-start = ((f32[16,40,128]{2,1,0:T(8,128)}), f32[16,40,128]{2,1,0:T(8,128)S(1)}, u32[]{:S(2)}, u32[]{:S(2)}) async-start(f32[16,40,128]{2,1,0:T(8,128)} %get-tuple-element.13), calls=%async_computation | async-start | bytes 655360 | tf_op jit(solution)/shard_map/all_to_all | solution.py:404
  20.1 0.0 copy-start
  20.1 2.1 %collective-permute-start.2 = (f32[5,1,1152]{2,1,0:T(1,128)S(1)}, f32[5,1,1152]{2,1,0:T(1,128)S(1)}, u32[]{:S(2)}, u32[]{:S(2)}) collective-permute-start(f32[5,1,1152]{2,1,0:T(1,128)S(1)} %get-tuple-element.14), channel_id=1, source_target_pairs={{0,512},{16,528},{32,544},{48,560},{64,576},{80,592},{96,608},{112... | collective-permute-start | bytes 69128 | tf_op jit(solution)/shard_map/ppermute | solution.py:379
  22.2 0.0 copy-done.3
  22.2 0.6 %fusion = (s32[1,1]{1,0:T(1,128)}, s32[1,1]{1,0:T(1,128)}) fusion(s32[1,8]{1,0:T(1,128)S(1)} %bitcast.21), kind=kLoop, calls=%fused_computation.2 | loop fusion | bytes 16 | tf_op jit(solution)/shard_map/slice | solution.py:412
  24.1 9.1 %all-to-all-done.received_ref = f32[16,40,128]{2,1,0:T(8,128)S(1)} async-done(((f32[16,40,128]{2,1,0:T(8,128)}), f32[16,40,128]{2,1,0:T(8,128)S(1)}, u32[]{:S(2)}, u32[]{:S(2)}) %all-to-all-start) | async-done | bytes 327712 | tf_op jit(solution)/shard_map/all_to_all | solution.py:404
  33.2 0.0 collective-permute-start
  33.2 0.5 %collective-permute-start.1 = (f32[20,128]{1,0:T(8,128)S(1)}, f32[20,128]{1,0:T(8,128)S(1)}, u32[]{:S(2)}, u32[]{:S(2)}) collective-permute-start(f32[20,128]{1,0:T(8,128)S(1)} %get-tuple-element.28), channel_id=1, source_target_pairs={{0,15},{1,0},{2,1},{3,2},{4,3},{5,4},{6,5},{7,6},{8,7},{9,8},{10,9... | collective-permute-start | bytes 30728 | tf_op jit(solution)/shard_map/ppermute | solution.py:379
  33.7 0.0 collective-permute-done.2.sides_ref
  33.7 0.0 copy-done.1
  33.7 0.0 copy-done.2
  33.7 0.4 ghosts.1
  34.1 0.0 copy-done
  34.1 1.6 %sides.1 = (f32[5,8,512]{2,1,0:T(8,128)S(1)}, f32[4,5,8,128]{3,2,1,0:T(8,128)S(1)}, f32[5,1,800]{2,1,0:T(1,128)S(1)}) custom-call(s32[1,8]{1,0:T(1,128)S(1)} %bitcast.22, f32[16,40,128]{2,1,0:T(8,128)S(1)} %all-to-all-done.received_ref, f32[5,3,8,128]{3,2,1,0:T(8,128)S(1)} %get-tuple-element.15.ghosts_ref, f32[5,8,128]{2,1,0:T(8,128)S(1)} %get-tuple-element.16.base_ref, ...), custom_call_target="tpu_custom_call" | custom-call | flops 50000000 | bytes 500000 | tf_op jit(solution)/shard_map/sides/pallas_call | solution.py:417
  35.7 0.0 collective-permute-done.before_ref
  35.7 0.9 %collective-permute-done.1.after_ref = f32[20,128]{1,0:T(8,128)S(1)} collective-permute-done((f32[20,128]{1,0:T(8,128)S(1)}, f32[20,128]{1,0:T(8,128)S(1)}, u32[]{:S(2)}, u32[]{:S(2)}) %collective-permute-start.1) | collective-permute-done | bytes 10272 | tf_op jit(solution)/shard_map/ppermute | solution.py:379
  36.6 0.4 edges.1
  37.0 7.2 %all-gather = f32[10,1,800]{2,1,0:T(1,128)S(1)} all-gather(f32[5,1,800]{2,1,0:T(1,128)S(1)} %get-tuple-element.21), channel_id=2, replica_groups={{0,512},{16,528},{32,544},{48,560},{64,576},{80,592},{96,608},{112,624}..., dimensions={0}, use_global_device_ids=true | all-gather | bytes 48000 | tf_op jit(solution)/shard_map/all_gather | solution.py:429
  44.1 0.7 %store.1 = (f32[5,8,512]{2,1,0:T(8,128)}, f32[5,1,800]{2,1,0:T(1,128)}) custom-call(f32[5,8,512]{2,1,0:T(8,128)S(1)} %get-tuple-element.20.fine_ref, f32[2,5,1,800]{3,2,1,0:T(1,128)S(1)} %bitcast.20), custom_call_target="tpu_custom_call" | custom-call | flops 1000000 | bytes 500000 | tf_op jit(solution)/shard_map/store/pallas_call | solution.py:430
  (1 shorter events, 0.0 us)
Async XLA Ops:
  2.5 19.7 %copy-start.3 = (s32[1,1,8]{2,1,0:T(1,128)S(1)}, s32[1,1,8]{2,1,0:T(1,128)}, u32[]{:S(2)}) copy-start(s32[1,1,8]{2,1,0:T(1,128)} %param.10) | copy-start | bytes 100
  2.5 31.2 %copy-start.1 = (f32[128,384]{1,0:T(8,128)S(1)}, f32[128,384]{1,0:T(8,128)}, u32[]{:S(2)}) copy-start(f32[128,384]{1,0:T(8,128)} %constant.14.clone.ghost_m_ref) | copy-start | bytes 589828
  2.5 31.2 %copy-start.2 = (f32[128,128]{1,0:T(8,128)S(1)}, f32[128,128]{1,0:T(8,128)}, u32[]{:S(2)}) copy-start(f32[128,128]{1,0:T(8,128)} %constant.16.clone.register_m_ref) | copy-start | bytes 196612
  2.5 30.7 %all-to-all-start = ((f32[16,40,128]{2,1,0:T(8,128)}), f32[16,40,128]{2,1,0:T(8,128)S(1)}, u32[]{:S(2)}, u32[]{:S(2)}) async-start(f32[16,40,128]{2,1,0:T(8,128)} %get-tuple-element.13), calls=%async_computation | async-start | bytes 655360 | tf_op jit(solution)/shard_map/all_to_all | solution.py:404
  20.1 14.0 %copy-start = (f32[640,128]{1,0:T(8,128)S(1)}, f32[640,128]{1,0:T(8,128)}, u32[]{:S(2)}) copy-start(f32[640,128]{1,0:T(8,128)} %constant.15.clone.mean_ref) | copy-start | bytes 983044
  20.1 13.6 %collective-permute-start.2 = (f32[5,1,1152]{2,1,0:T(1,128)S(1)}, f32[5,1,1152]{2,1,0:T(1,128)S(1)}, u32[]{:S(2)}, u32[]{:S(2)}) collective-permute-start(f32[5,1,1152]{2,1,0:T(1,128)S(1)} %get-tuple-element.14), channel_id=1, source_target_pairs={{0,512},{16,528},{32,544},{48,560},{64,576},{80,592},{96,608},{112... | collective-permute-start | bytes 69128 | tf_op jit(solution)/shard_map/ppermute | solution.py:379
  33.2 2.5 %collective-permute-start = (f32[20,128]{1,0:T(8,128)S(1)}, f32[20,128]{1,0:T(8,128)S(1)}, u32[]{:S(2)}, u32[]{:S(2)}) collective-permute-start(f32[20,128]{1,0:T(8,128)S(1)} %get-tuple-element.29), channel_id=1, source_target_pairs={{0,1},{1,2},{2,3},{3,4},{4,5},{5,6},{6,7},{7,8},{8,9},{9,10},{10,1... | collective-permute-start | bytes 30728 | tf_op jit(solution)/shard_map/ppermute | solution.py:379
  33.2 3.4 %collective-permute-start.1 = (f32[20,128]{1,0:T(8,128)S(1)}, f32[20,128]{1,0:T(8,128)S(1)}, u32[]{:S(2)}, u32[]{:S(2)}) collective-permute-start(f32[20,128]{1,0:T(8,128)S(1)} %get-tuple-element.28), channel_id=1, source_target_pairs={{0,15},{1,0},{2,1},{3,2},{4,3},{5,4},{6,5},{7,6},{8,7},{9,8},{10,9... | collective-permute-start | bytes 30728 | tf_op jit(solution)/shard_map/ppermute | solution.py:379

commit v5 on v4

--- a/solution.py
+++ b/solution.py
@@ -420,7 +420,7 @@
         [S, V, V, V, V],
         "sides",
         50_000_000,
-        [pltpu.VMEM((8 * STRIDE, LANES), jnp.float32)],
+        [pltpu.VMEM((9 * STRIDE, LANES), jnp.float32)],
     )(arrive, received.reshape(peers, 2 * ROWS, LANES), ghosts, base, mean_m)
     fine, block_new = call(
         edge_kernel, [fine_shape, block_shape], [V] * 6, "edges", 20_000_000

time: 45.1 us -> 45.1 us (level)
  no operation moved by 1% of the time
where the time goes in v5:
time: 45.1 us; the launch traced here: 44.8 us
  starting transfers between devices  20.2 us (45%)
  waiting for transfers between devices  9.96 us (22%)
  blocking collectives  7.19 us (16%)
  Pallas kernels  4.8 us (11%)
  between operations  2.04 us (5%)
  local copies, waits for them, and re-layouts  0.62 us (1%)
    all_to_all x1, starting transfers between devices, local(): lax.all_to_all(outgoing, 'gy', split_axis=0, concat_axis=0, tiled=True)  17.6 us
    all_to_all x1, waiting for transfers between devices, local(): lax.all_to_all(outgoing, 'gy', split_axis=0, concat_axis=0, tiled=True)  9.07 us
    all_gather x1, blocking collectives, local(): both = lax.all_gather(block_new, 'gx', axis_index_groups=pairs)  7.19 us
    ppermute x3, starting transfers between devices, passed_along(): lax.ppermute(value, axis, [(source, (source + steps) % count) for source...  2.57 us
    pallas_call x1, Pallas kernels, local(): call(pack_kernel, [(peers, 2 * ROWS, LANES), (NF, 1, FACES_AT + register....  1.84 us
    pallas_call x1, Pallas kernels, local(): call(side_kernel, [fine_shape, (4, NF, 8, LANES), block_shape], [S, V, V,...  1.55 us
  transfers between devices with their start and end apart: 4, of which 2 were waited for; matrix products, arithmetic and copies ran while one was open for 1% of the time, Pallas kernels for 4%

profile of v5, /device:TPU:1, one launch (start us, length us, event | category | flops | bytes accessed | tf_op | source)
XLA Modules:
  0.0 44.8 jit_solution(8813243391046822483)
XLA Ops:
  0.6 1.8 %pack.1 = (f32[16,40,128]{2,1,0:T(8,128)}, f32[5,1,1152]{2,1,0:T(1,128)S(1)}) custom-call(s32[2,16]{1,0:T(2,128)} %bitcast.26, f32[5,16,512]{2,1,0:T(8,128)} %bitcast.23, f32[5,1,800]{2,1,0:T(1,128)} %bitcast.24, f32[5,1,256]{2,1,0:T(1,128)} %bitcast.25), custom_call_target="tpu_custom_call" | custom-call | flops 1000000 | bytes 500000 | tf_op jit(solution)/shard_map/pack/pallas_call | solution.py:390
  2.5 0.0 copy-start.3
  2.5 0.0 copy-start.1
  2.5 0.0 copy-start.2
  2.5 17.6 %all-to-all-start = ((f32[16,40,128]{2,1,0:T(8,128)}), f32[16,40,128]{2,1,0:T(8,128)S(1)}, u32[]{:S(2)}, u32[]{:S(2)}) async-start(f32[16,40,128]{2,1,0:T(8,128)} %get-tuple-element.13), calls=%async_computation | async-start | bytes 655360 | tf_op jit(solution)/shard_map/all_to_all | solution.py:404
  20.1 0.0 copy-start
  20.1 2.1 %collective-permute-start.2 = (f32[5,1,1152]{2,1,0:T(1,128)S(1)}, f32[5,1,1152]{2,1,0:T(1,128)S(1)}, u32[]{:S(2)}, u32[]{:S(2)}) collective-permute-start(f32[5,1,1152]{2,1,0:T(1,128)S(1)} %get-tuple-element.14), channel_id=1, source_target_pairs={{0,512},{16,528},{32,544},{48,560},{64,576},{80,592},{96,608},{112... | collective-permute-start | bytes 69128 | tf_op jit(solution)/shard_map/ppermute | solution.py:379
  22.2 0.0 copy-done.3
  22.2 0.6 %fusion = (s32[1,1]{1,0:T(1,128)}, s32[1,1]{1,0:T(1,128)}) fusion(s32[1,8]{1,0:T(1,128)S(1)} %bitcast.21), kind=kLoop, calls=%fused_computation.2 | loop fusion | bytes 16 | tf_op jit(solution)/shard_map/slice | solution.py:412
  24.1 9.1 %all-to-all-done.received_ref = f32[16,40,128]{2,1,0:T(8,128)S(1)} async-done(((f32[16,40,128]{2,1,0:T(8,128)}), f32[16,40,128]{2,1,0:T(8,128)S(1)}, u32[]{:S(2)}, u32[]{:S(2)}) %all-to-all-start) | async-done | bytes 327712 | tf_op jit(solution)/shard_map/all_to_all | solution.py:404
  33.2 0.0 collective-permute-start
  33.2 0.5 %collective-permute-start.1 = (f32[20,128]{1,0:T(8,128)S(1)}, f32[20,128]{1,0:T(8,128)S(1)}, u32[]{:S(2)}, u32[]{:S(2)}) collective-permute-start(f32[20,128]{1,0:T(8,128)S(1)} %get-tuple-element.28), channel_id=1, source_target_pairs={{0,15},{1,0},{2,1},{3,2},{4,3},{5,4},{6,5},{7,6},{8,7},{9,8},{10,9... | collective-permute-start | bytes 30728 | tf_op jit(solution)/shard_map/ppermute | solution.py:379
  33.7 0.0 collective-permute-done.2.sides_ref
  33.7 0.0 copy-done.1
  33.7 0.0 copy-done.2
  33.7 0.4 ghosts.1
  34.1 0.0 copy-done
  34.1 1.6 %sides.1 = (f32[5,8,512]{2,1,0:T(8,128)S(1)}, f32[4,5,8,128]{3,2,1,0:T(8,128)S(1)}, f32[5,1,800]{2,1,0:T(1,128)S(1)}) custom-call(s32[1,8]{1,0:T(1,128)S(1)} %bitcast.22, f32[16,40,128]{2,1,0:T(8,128)S(1)} %all-to-all-done.received_ref, f32[5,3,8,128]{3,2,1,0:T(8,128)S(1)} %get-tuple-element.15.ghosts_ref, f32[5,8,128]{2,1,0:T(8,128)S(1)} %get-tuple-element.16.base_ref, ...), custom_call_target="tpu_custom_call" | custom-call | flops 50000000 | bytes 500000 | tf_op jit(solution)/shard_map/sides/pallas_call | solution.py:417
  35.7 0.0 collective-permute-done.before_ref
  35.7 0.9 %collective-permute-done.1.after_ref = f32[20,128]{1,0:T(8,128)S(1)} collective-permute-done((f32[20,128]{1,0:T(8,128)S(1)}, f32[20,128]{1,0:T(8,128)S(1)}, u32[]{:S(2)}, u32[]{:S(2)}) %collective-permute-start.1) | collective-permute-done | bytes 10272 | tf_op jit(solution)/shard_map/ppermute | solution.py:379
  36.6 0.4 edges.1
  37.0 7.2 %all-gather = f32[10,1,800]{2,1,0:T(1,128)S(1)} all-gather(f32[5,1,800]{2,1,0:T(1,128)S(1)} %get-tuple-element.21), channel_id=2, replica_groups={{0,512},{16,528},{32,544},{48,560},{64,576},{80,592},{96,608},{112,624}..., dimensions={0}, use_global_device_ids=true | all-gather | bytes 48000 | tf_op jit(solution)/shard_map/all_gather | solution.py:429
  44.1 0.7 %store.1 = (f32[5,8,512]{2,1,0:T(8,128)}, f32[5,1,800]{2,1,0:T(1,128)}) custom-call(f32[5,8,512]{2,1,0:T(8,128)S(1)} %get-tuple-element.20.fine_ref, f32[2,5,1,800]{3,2,1,0:T(1,128)S(1)} %bitcast.20), custom_call_target="tpu_custom_call" | custom-call | flops 1000000 | bytes 500000 | tf_op jit(solution)/shard_map/store/pallas_call | solution.py:430
  (1 shorter events, 0.0 us)
Async XLA Ops:
  2.5 19.7 %copy-start.3 = (s32[1,1,8]{2,1,0:T(1,128)S(1)}, s32[1,1,8]{2,1,0:T(1,128)}, u32[]{:S(2)}) copy-start(s32[1,1,8]{2,1,0:T(1,128)} %param.10) | copy-start | bytes 100
  2.5 31.2 %copy-start.1 = (f32[128,384]{1,0:T(8,128)S(1)}, f32[128,384]{1,0:T(8,128)}, u32[]{:S(2)}) copy-start(f32[128,384]{1,0:T(8,128)} %constant.14.clone.ghost_m_ref) | copy-start | bytes 589828
  2.5 31.2 %copy-start.2 = (f32[128,128]{1,0:T(8,128)S(1)}, f32[128,128]{1,0:T(8,128)}, u32[]{:S(2)}) copy-start(f32[128,128]{1,0:T(8,128)} %constant.16.clone.register_m_ref) | copy-start | bytes 196612
  2.5 30.7 %all-to-all-start = ((f32[16,40,128]{2,1,0:T(8,128)}), f32[16,40,128]{2,1,0:T(8,128)S(1)}, u32[]{:S(2)}, u32[]{:S(2)}) async-start(f32[16,40,128]{2,1,0:T(8,128)} %get-tuple-element.13), calls=%async_computation | async-start | bytes 655360 | tf_op jit(solution)/shard_map/all_to_all | solution.py:404
  20.1 14.0 %copy-start = (f32[640,128]{1,0:T(8,128)S(1)}, f32[640,128]{1,0:T(8,128)}, u32[]{:S(2)}) copy-start(f32[640,128]{1,0:T(8,128)} %constant.15.clone.mean_ref) | copy-start | bytes 983044
  20.1 13.6 %collective-permute-start.2 = (f32[5,1,1152]{2,1,0:T(1,128)S(1)}, f32[5,1,1152]{2,1,0:T(1,128)S(1)}, u32[]{:S(2)}, u32[]{:S(2)}) collective-permute-start(f32[5,1,1152]{2,1,0:T(1,128)S(1)} %get-tuple-element.14), channel_id=1, source_target_pairs={{0,512},{16,528},{32,544},{48,560},{64,576},{80,592},{96,608},{112... | collective-permute-start | bytes 69128 | tf_op jit(solution)/shard_map/ppermute | solution.py:379
  33.2 2.5 %collective-permute-start = (f32[20,128]{1,0:T(8,128)S(1)}, f32[20,128]{1,0:T(8,128)S(1)}, u32[]{:S(2)}, u32[]{:S(2)}) collective-permute-start(f32[20,128]{1,0:T(8,128)S(1)} %get-tuple-element.29), channel_id=1, source_target_pairs={{0,1},{1,2},{2,3},{3,4},{4,5},{5,6},{6,7},{7,8},{8,9},{9,10},{10,1... | collective-permute-start | bytes 30728 | tf_op jit(solution)/shard_map/ppermute | solution.py:379
  33.2 3.4 %collective-permute-start.1 = (f32[20,128]{1,0:T(8,128)S(1)}, f32[20,128]{1,0:T(8,128)S(1)}, u32[]{:S(2)}, u32[]{:S(2)}) collective-permute-start(f32[20,128]{1,0:T(8,128)S(1)} %get-tuple-element.28), channel_id=1, source_target_pairs={{0,15},{1,0},{2,1},{3,2},{4,3},{5,4},{6,5},{7,6},{8,7},{9,8},{10,9... | collective-permute-start | bytes 30728 | tf_op jit(solution)/shard_map/ppermute | solution.py:379

commit v6 on v5

--- a/solution.py
+++ b/solution.py
@@ -318,13 +318,18 @@
         lower.append(low + 0.5 * minmod(low - under, step))
         upper.append(high - 0.5 * minmod(step, over - high))
     flux = face_flux(lower, upper, 2)
-    stacked = jnp.concatenate(flux, axis=0)
-    means = [
-        jnp.dot(
-            stacked, mean_ref[h * LANES : (h + 1) * LANES], precision=HIGHEST, preferred_element_type=jnp.float32
-        )
-        for h in range(2)
-    ]
+    rest, parts = (jnp.concatenate(flux, axis=0), [])
+    for _ in range(3):
+        parts.append(rest.astype(jnp.bfloat16))
+        rest = rest - parts[-1].astype(jnp.float32)
+    weights = jnp.concatenate(
+        [mean_ref[h * LANES : (h + 1) * LANES].astype(jnp.bfloat16) for h in range(2)], axis=1
+    )
+    stacked = jnp.concatenate(parts, axis=0)
+    product = jnp.dot(stacked, weights, preferred_element_type=jnp.float32)
+    count = 8 * NF
+    product = product[:count] + product[count : 2 * count] + product[2 * count :]
+    means = [product[:, h * LANES : (h + 1) * LANES] for h in range(2)]
     tail = 8 * CYCLE - 6 * LANES
     for f in range(NF):
         above = jnp.where(row < 2, pltpu.roll(flux[f], 6, 0), jnp.where(row < 4, 0.0, flux[f]))

time: 45.1 us -> 45 us (level)
  no operation moved by 1% of the time
where the time goes in v6:
time: 45 us; the launch traced here: 44.7 us
  starting transfers between devices  20.2 us (45%)
  waiting for transfers between devices  9.96 us (22%)
  blocking collectives  7.19 us (16%)
  Pallas kernels  4.7 us (10%)
  between operations  2.04 us (5%)
  local copies, waits for them, and re-layouts  0.62 us (1%)
    all_to_all x1, starting transfers between devices, local(): lax.all_to_all(outgoing, 'gy', split_axis=0, concat_axis=0, tiled=True)  17.6 us
    all_to_all x1, waiting for transfers between devices, local(): lax.all_to_all(outgoing, 'gy', split_axis=0, concat_axis=0, tiled=True)  9.07 us
    all_gather x1, blocking collectives, local(): both = lax.all_gather(block_new, 'gx', axis_index_groups=pairs)  7.19 us
    ppermute x3, starting transfers between devices, passed_along(): lax.ppermute(value, axis, [(source, (source + steps) % count) for source...  2.57 us
    pallas_call x1, Pallas kernels, local(): call(pack_kernel, [(peers, 2 * ROWS, LANES), (NF, 1, FACES_AT + register....  1.84 us
    pallas_call x1, Pallas kernels, local(): call(side_kernel, [fine_shape, (4, NF, 8, LANES), block_shape], [S, V, V,...  1.55 us
  transfers between devices with their start and end apart: 4, of which 2 were waited for; matrix products, arithmetic and copies ran while one was open for 1% of the time, Pallas kernels for 4%

profile of v6, /device:TPU:1, one launch (start us, length us, event | category | flops | bytes accessed | tf_op | source)
XLA Modules:
  0.0 44.7 jit_solution(7834673222751557537)
XLA Ops:
  0.6 1.8 %pack.1 = (f32[16,40,128]{2,1,0:T(8,128)}, f32[5,1,1152]{2,1,0:T(1,128)S(1)}) custom-call(s32[2,16]{1,0:T(2,128)} %bitcast.26, f32[5,16,512]{2,1,0:T(8,128)} %bitcast.23, f32[5,1,800]{2,1,0:T(1,128)} %bitcast.24, f32[5,1,256]{2,1,0:T(1,128)} %bitcast.25), custom_call_target="tpu_custom_call" | custom-call | flops 1000000 | bytes 500000 | tf_op jit(solution)/shard_map/pack/pallas_call | solution.py:395
  2.5 0.0 copy-start.3
  2.5 0.0 copy-start.1
  2.5 0.0 copy-start.2
  2.5 17.6 %all-to-all-start = ((f32[16,40,128]{2,1,0:T(8,128)}), f32[16,40,128]{2,1,0:T(8,128)S(1)}, u32[]{:S(2)}, u32[]{:S(2)}) async-start(f32[16,40,128]{2,1,0:T(8,128)} %get-tuple-element.13), calls=%async_computation | async-start | bytes 655360 | tf_op jit(solution)/shard_map/all_to_all | solution.py:409
  20.1 0.0 copy-start
  20.1 2.1 %collective-permute-start.2 = (f32[5,1,1152]{2,1,0:T(1,128)S(1)}, f32[5,1,1152]{2,1,0:T(1,128)S(1)}, u32[]{:S(2)}, u32[]{:S(2)}) collective-permute-start(f32[5,1,1152]{2,1,0:T(1,128)S(1)} %get-tuple-element.14), channel_id=1, source_target_pairs={{0,512},{16,528},{32,544},{48,560},{64,576},{80,592},{96,608},{112... | collective-permute-start | bytes 69128 | tf_op jit(solution)/shard_map/ppermute | solution.py:384
  22.2 0.0 copy-done.3
  22.2 0.6 %fusion = (s32[1,1]{1,0:T(1,128)}, s32[1,1]{1,0:T(1,128)}) fusion(s32[1,8]{1,0:T(1,128)S(1)} %bitcast.21), kind=kLoop, calls=%fused_computation.2 | loop fusion | bytes 16 | tf_op jit(solution)/shard_map/slice | solution.py:417
  24.1 9.1 %all-to-all-done.received_ref = f32[16,40,128]{2,1,0:T(8,128)S(1)} async-done(((f32[16,40,128]{2,1,0:T(8,128)}), f32[16,40,128]{2,1,0:T(8,128)S(1)}, u32[]{:S(2)}, u32[]{:S(2)}) %all-to-all-start) | async-done | bytes 327712 | tf_op jit(solution)/shard_map/all_to_all | solution.py:409
  33.2 0.0 collective-permute-start
  33.2 0.5 %collective-permute-start.1 = (f32[20,128]{1,0:T(8,128)S(1)}, f32[20,128]{1,0:T(8,128)S(1)}, u32[]{:S(2)}, u32[]{:S(2)}) collective-permute-start(f32[20,128]{1,0:T(8,128)S(1)} %get-tuple-element.28), channel_id=1, source_target_pairs={{0,15},{1,0},{2,1},{3,2},{4,3},{5,4},{6,5},{7,6},{8,7},{9,8},{10,9... | collective-permute-start | bytes 30728 | tf_op jit(solution)/shard_map/ppermute | solution.py:384
  33.7 0.0 collective-permute-done.2.sides_ref
  33.7 0.0 copy-done.1
  33.7 0.0 copy-done.2
  33.7 0.4 ghosts.1
  34.1 0.0 copy-done
  34.1 1.6 %sides.1 = (f32[5,8,512]{2,1,0:T(8,128)S(1)}, f32[4,5,8,128]{3,2,1,0:T(8,128)S(1)}, f32[5,1,800]{2,1,0:T(1,128)S(1)}) custom-call(s32[1,8]{1,0:T(1,128)S(1)} %bitcast.22, f32[16,40,128]{2,1,0:T(8,128)S(1)} %all-to-all-done.received_ref, f32[5,3,8,128]{3,2,1,0:T(8,128)S(1)} %get-tuple-element.15.ghosts_ref, f32[5,8,128]{2,1,0:T(8,128)S(1)} %get-tuple-element.16.base_ref, ...), custom_call_target="tpu_custom_call" | custom-call | flops 50000000 | bytes 500000 | tf_op jit(solution)/shard_map/sides/pallas_call | solution.py:422
  35.7 0.0 collective-permute-done.before_ref
  35.7 0.9 %collective-permute-done.1.after_ref = f32[20,128]{1,0:T(8,128)S(1)} collective-permute-done((f32[20,128]{1,0:T(8,128)S(1)}, f32[20,128]{1,0:T(8,128)S(1)}, u32[]{:S(2)}, u32[]{:S(2)}) %collective-permute-start.1) | collective-permute-done | bytes 10272 | tf_op jit(solution)/shard_map/ppermute | solution.py:384
  36.6 0.3 edges.1
  36.9 7.2 %all-gather = f32[10,1,800]{2,1,0:T(1,128)S(1)} all-gather(f32[5,1,800]{2,1,0:T(1,128)S(1)} %get-tuple-element.21), channel_id=2, replica_groups={{0,512},{16,528},{32,544},{48,560},{64,576},{80,592},{96,608},{112,624}..., dimensions={0}, use_global_device_ids=true | all-gather | bytes 48000 | tf_op jit(solution)/shard_map/all_gather | solution.py:434
  44.0 0.7 %store.1 = (f32[5,8,512]{2,1,0:T(8,128)}, f32[5,1,800]{2,1,0:T(1,128)}) custom-call(f32[5,8,512]{2,1,0:T(8,128)S(1)} %get-tuple-element.20.fine_ref, f32[2,5,1,800]{3,2,1,0:T(1,128)S(1)} %bitcast.20), custom_call_target="tpu_custom_call" | custom-call | flops 1000000 | bytes 500000 | tf_op jit(solution)/shard_map/store/pallas_call | solution.py:435
  (1 shorter events, 0.0 us)
Async XLA Ops:
  2.5 19.7 %copy-start.3 = (s32[1,1,8]{2,1,0:T(1,128)S(1)}, s32[1,1,8]{2,1,0:T(1,128)}, u32[]{:S(2)}) copy-start(s32[1,1,8]{2,1,0:T(1,128)} %param.10) | copy-start | bytes 100
  2.5 31.2 %copy-start.1 = (f32[128,384]{1,0:T(8,128)S(1)}, f32[128,384]{1,0:T(8,128)}, u32[]{:S(2)}) copy-start(f32[128,384]{1,0:T(8,128)} %constant.14.clone.ghost_m_ref) | copy-start | bytes 589828
  2.5 31.2 %copy-start.2 = (f32[128,128]{1,0:T(8,128)S(1)}, f32[128,128]{1,0:T(8,128)}, u32[]{:S(2)}) copy-start(f32[128,128]{1,0:T(8,128)} %constant.16.clone.register_m_ref) | copy-start | bytes 196612
  2.5 30.7 %all-to-all-start = ((f32[16,40,128]{2,1,0:T(8,128)}), f32[16,40,128]{2,1,0:T(8,128)S(1)}, u32[]{:S(2)}, u32[]{:S(2)}) async-start(f32[16,40,128]{2,1,0:T(8,128)} %get-tuple-element.13), calls=%async_computation | async-start | bytes 655360 | tf_op jit(solution)/shard_map/all_to_all | solution.py:409
  20.1 14.0 %copy-start = (f32[640,128]{1,0:T(8,128)S(1)}, f32[640,128]{1,0:T(8,128)}, u32[]{:S(2)}) copy-start(f32[640,128]{1,0:T(8,128)} %constant.15.clone.mean_ref) | copy-start | bytes 983044
  20.1 13.6 %collective-permute-start.2 = (f32[5,1,1152]{2,1,0:T(1,128)S(1)}, f32[5,1,1152]{2,1,0:T(1,128)S(1)}, u32[]{:S(2)}, u32[]{:S(2)}) collective-permute-start(f32[5,1,1152]{2,1,0:T(1,128)S(1)} %get-tuple-element.14), channel_id=1, source_target_pairs={{0,512},{16,528},{32,544},{48,560},{64,576},{80,592},{96,608},{112... | collective-permute-start | bytes 69128 | tf_op jit(solution)/shard_map/ppermute | solution.py:384
  33.2 2.5 %collective-permute-start = (f32[20,128]{1,0:T(8,128)S(1)}, f32[20,128]{1,0:T(8,128)S(1)}, u32[]{:S(2)}, u32[]{:S(2)}) collective-permute-start(f32[20,128]{1,0:T(8,128)S(1)} %get-tuple-element.29), channel_id=1, source_target_pairs={{0,1},{1,2},{2,3},{3,4},{4,5},{5,6},{6,7},{7,8},{8,9},{9,10},{10,1... | collective-permute-start | bytes 30728 | tf_op jit(solution)/shard_map/ppermute | solution.py:384
  33.2 3.4 %collective-permute-start.1 = (f32[20,128]{1,0:T(8,128)S(1)}, f32[20,128]{1,0:T(8,128)S(1)}, u32[]{:S(2)}, u32[]{:S(2)}) collective-permute-start(f32[20,128]{1,0:T(8,128)S(1)} %get-tuple-element.28), channel_id=1, source_target_pairs={{0,15},{1,0},{2,1},{3,2},{4,3},{5,4},{6,5},{7,6},{8,7},{9,8},{10,9... | collective-permute-start | bytes 30728 | tf_op jit(solution)/shard_map/ppermute | solution.py:384

commit v7 on v6

--- a/solution.py
+++ b/solution.py
@@ -94,18 +94,20 @@
 def pack_kernel(slots_hbm, boxes_hbm, coarse_hbm, flux_hbm, out_ref, sides_ref, slots_ref, boxes_ref, coarse_ref, flux_ref, sems):
     cells, faces = (coarse_hbm.shape[2], flux_hbm.shape[2])
     copies = [
-        pltpu.make_async_copy(slots_hbm, slots_ref, sems.at[0]),
-        pltpu.make_async_copy(boxes_hbm, boxes_ref, sems.at[1]),
+        pltpu.make_async_copy(slots_hbm, slots_ref, sems.at[1]),
+        pltpu.make_async_copy(boxes_hbm, boxes_ref, sems.at[0]),
         pltpu.make_async_copy(coarse_hbm, coarse_ref, sems.at[2]),
         pltpu.make_async_copy(flux_hbm, flux_ref, sems.at[3]),
     ]
     for one in copies:
         one.start()
-    for one in copies:
+    for one in copies[2:]:
         one.wait()
     for f in range(NF):
         sides_ref[f, :, pl.ds(0, cells)] = coarse_ref[f]
         sides_ref[f, :, pl.ds(FACES_AT, faces)] = flux_ref[f]
+    for one in copies[:2]:
+        one.wait()
     held = boxes_ref.shape[1]
     row = lax.broadcasted_iota(jnp.int32, (8, LANES), 0)
 

time: 45 us -> 45 us (level)
  no operation moved by 1% of the time
where the time goes in v7:
time: 45 us; the launch traced here: 44.7 us
  starting transfers between devices  20.2 us (45%)
  waiting for transfers between devices  9.96 us (22%)
  blocking collectives  7.19 us (16%)
  Pallas kernels  4.69 us (10%)
  between operations  2.04 us (5%)
  local copies, waits for them, and re-layouts  0.62 us (1%)
    all_to_all x1, starting transfers between devices, local(): lax.all_to_all(outgoing, 'gy', split_axis=0, concat_axis=0, tiled=True)  17.6 us
    all_to_all x1, waiting for transfers between devices, local(): lax.all_to_all(outgoing, 'gy', split_axis=0, concat_axis=0, tiled=True)  9.07 us
    all_gather x1, blocking collectives, local(): both = lax.all_gather(block_new, 'gx', axis_index_groups=pairs)  7.19 us
    ppermute x3, starting transfers between devices, passed_along(): lax.ppermute(value, axis, [(source, (source + steps) % count) for source...  2.57 us
    pallas_call x1, Pallas kernels, local(): call(pack_kernel, [(peers, 2 * ROWS, LANES), (NF, 1, FACES_AT + register....  1.83 us
    pallas_call x1, Pallas kernels, local(): call(side_kernel, [fine_shape, (4, NF, 8, LANES), block_shape], [S, V, V,...  1.55 us
  transfers between devices with their start and end apart: 4, of which 2 were waited for; matrix products, arithmetic and copies ran while one was open for 1% of the time, Pallas kernels for 4%

profile of v7, /device:TPU:1, one launch (start us, length us, event | category | flops | bytes accessed | tf_op | source)
XLA Modules:
  0.0 44.7 jit_solution(346322849800158219)
XLA Ops:
  0.6 1.8 %pack.1 = (f32[16,40,128]{2,1,0:T(8,128)}, f32[5,1,1152]{2,1,0:T(1,128)S(1)}) custom-call(s32[2,16]{1,0:T(2,128)} %bitcast.26, f32[5,16,512]{2,1,0:T(8,128)} %bitcast.23, f32[5,1,800]{2,1,0:T(1,128)} %bitcast.24, f32[5,1,256]{2,1,0:T(1,128)} %bitcast.25), custom_call_target="tpu_custom_call" | custom-call | flops 1000000 | bytes 500000 | tf_op jit(solution)/shard_map/pack/pallas_call | solution.py:397
  2.5 0.0 copy-start.3
  2.5 0.0 copy-start.1
  2.5 0.0 copy-start.2
  2.5 17.6 %all-to-all-start = ((f32[16,40,128]{2,1,0:T(8,128)}), f32[16,40,128]{2,1,0:T(8,128)S(1)}, u32[]{:S(2)}, u32[]{:S(2)}) async-start(f32[16,40,128]{2,1,0:T(8,128)} %get-tuple-element.13), calls=%async_computation | async-start | bytes 655360 | tf_op jit(solution)/shard_map/all_to_all | solution.py:411
  20.1 0.0 copy-start
  20.1 2.1 %collective-permute-start.2 = (f32[5,1,1152]{2,1,0:T(1,128)S(1)}, f32[5,1,1152]{2,1,0:T(1,128)S(1)}, u32[]{:S(2)}, u32[]{:S(2)}) collective-permute-start(f32[5,1,1152]{2,1,0:T(1,128)S(1)} %get-tuple-element.14), channel_id=1, source_target_pairs={{0,512},{16,528},{32,544},{48,560},{64,576},{80,592},{96,608},{112... | collective-permute-start | bytes 69128 | tf_op jit(solution)/shard_map/ppermute | solution.py:386
  22.2 0.0 copy-done.3
  22.2 0.6 %fusion = (s32[1,1]{1,0:T(1,128)}, s32[1,1]{1,0:T(1,128)}) fusion(s32[1,8]{1,0:T(1,128)S(1)} %bitcast.21), kind=kLoop, calls=%fused_computation.2 | loop fusion | bytes 16 | tf_op jit(solution)/shard_map/slice | solution.py:419
  24.1 9.1 %all-to-all-done.received_ref = f32[16,40,128]{2,1,0:T(8,128)S(1)} async-done(((f32[16,40,128]{2,1,0:T(8,128)}), f32[16,40,128]{2,1,0:T(8,128)S(1)}, u32[]{:S(2)}, u32[]{:S(2)}) %all-to-all-start) | async-done | bytes 327712 | tf_op jit(solution)/shard_map/all_to_all | solution.py:411
  33.2 0.0 collective-permute-start
  33.2 0.5 %collective-permute-start.1 = (f32[20,128]{1,0:T(8,128)S(1)}, f32[20,128]{1,0:T(8,128)S(1)}, u32[]{:S(2)}, u32[]{:S(2)}) collective-permute-start(f32[20,128]{1,0:T(8,128)S(1)} %get-tuple-element.28), channel_id=1, source_target_pairs={{0,15},{1,0},{2,1},{3,2},{4,3},{5,4},{6,5},{7,6},{8,7},{9,8},{10,9... | collective-permute-start | bytes 30728 | tf_op jit(solution)/shard_map/ppermute | solution.py:386
  33.7 0.0 collective-permute-done.2.sides_ref
  33.7 0.0 copy-done.1
  33.7 0.0 copy-done.2
  33.7 0.4 ghosts.1
  34.1 0.0 copy-done
  34.1 1.6 %sides.1 = (f32[5,8,512]{2,1,0:T(8,128)S(1)}, f32[4,5,8,128]{3,2,1,0:T(8,128)S(1)}, f32[5,1,800]{2,1,0:T(1,128)S(1)}) custom-call(s32[1,8]{1,0:T(1,128)S(1)} %bitcast.22, f32[16,40,128]{2,1,0:T(8,128)S(1)} %all-to-all-done.received_ref, f32[5,3,8,128]{3,2,1,0:T(8,128)S(1)} %get-tuple-element.15.ghosts_ref, f32[5,8,128]{2,1,0:T(8,128)S(1)} %get-tuple-element.16.base_ref, ...), custom_call_target="tpu_custom_call" | custom-call | flops 50000000 | bytes 500000 | tf_op jit(solution)/shard_map/sides/pallas_call | solution.py:424
  35.7 0.0 collective-permute-done.before_ref
  35.7 0.9 %collective-permute-done.1.after_ref = f32[20,128]{1,0:T(8,128)S(1)} collective-permute-done((f32[20,128]{1,0:T(8,128)S(1)}, f32[20,128]{1,0:T(8,128)S(1)}, u32[]{:S(2)}, u32[]{:S(2)}) %collective-permute-start.1) | collective-permute-done | bytes 10272 | tf_op jit(solution)/shard_map/ppermute | solution.py:386
  36.6 0.3 edges.1
  36.8 7.2 %all-gather = f32[10,1,800]{2,1,0:T(1,128)S(1)} all-gather(f32[5,1,800]{2,1,0:T(1,128)S(1)} %get-tuple-element.21), channel_id=2, replica_groups={{0,512},{16,528},{32,544},{48,560},{64,576},{80,592},{96,608},{112,624}..., dimensions={0}, use_global_device_ids=true | all-gather | bytes 48000 | tf_op jit(solution)/shard_map/all_gather | solution.py:436
  44.0 0.7 %store.1 = (f32[5,8,512]{2,1,0:T(8,128)}, f32[5,1,800]{2,1,0:T(1,128)}) custom-call(f32[5,8,512]{2,1,0:T(8,128)S(1)} %get-tuple-element.20.fine_ref, f32[2,5,1,800]{3,2,1,0:T(1,128)S(1)} %bitcast.20), custom_call_target="tpu_custom_call" | custom-call | flops 1000000 | bytes 500000 | tf_op jit(solution)/shard_map/store/pallas_call | solution.py:437
  (1 shorter events, 0.0 us)
Async XLA Ops:
  2.5 19.7 %copy-start.3 = (s32[1,1,8]{2,1,0:T(1,128)S(1)}, s32[1,1,8]{2,1,0:T(1,128)}, u32[]{:S(2)}) copy-start(s32[1,1,8]{2,1,0:T(1,128)} %param.10) | copy-start | bytes 100
  2.5 31.2 %copy-start.1 = (f32[128,384]{1,0:T(8,128)S(1)}, f32[128,384]{1,0:T(8,128)}, u32[]{:S(2)}) copy-start(f32[128,384]{1,0:T(8,128)} %constant.14.clone.ghost_m_ref) | copy-start | bytes 589828
  2.5 31.2 %copy-start.2 = (f32[128,128]{1,0:T(8,128)S(1)}, f32[128,128]{1,0:T(8,128)}, u32[]{:S(2)}) copy-start(f32[128,128]{1,0:T(8,128)} %constant.16.clone.register_m_ref) | copy-start | bytes 196612
  2.5 30.7 %all-to-all-start = ((f32[16,40,128]{2,1,0:T(8,128)}), f32[16,40,128]{2,1,0:T(8,128)S(1)}, u32[]{:S(2)}, u32[]{:S(2)}) async-start(f32[16,40,128]{2,1,0:T(8,128)} %get-tuple-element.13), calls=%async_computation | async-start | bytes 655360 | tf_op jit(solution)/shard_map/all_to_all | solution.py:411
  20.1 14.0 %copy-start = (f32[640,128]{1,0:T(8,128)S(1)}, f32[640,128]{1,0:T(8,128)}, u32[]{:S(2)}) copy-start(f32[640,128]{1,0:T(8,128)} %constant.15.clone.mean_ref) | copy-start | bytes 983044
  20.1 13.6 %collective-permute-start.2 = (f32[5,1,1152]{2,1,0:T(1,128)S(1)}, f32[5,1,1152]{2,1,0:T(1,128)S(1)}, u32[]{:S(2)}, u32[]{:S(2)}) collective-permute-start(f32[5,1,1152]{2,1,0:T(1,128)S(1)} %get-tuple-element.14), channel_id=1, source_target_pairs={{0,512},{16,528},{32,544},{48,560},{64,576},{80,592},{96,608},{112... | collective-permute-start | bytes 69128 | tf_op jit(solution)/shard_map/ppermute | solution.py:386
  33.2 2.5 %collective-permute-start = (f32[20,128]{1,0:T(8,128)S(1)}, f32[20,128]{1,0:T(8,128)S(1)}, u32[]{:S(2)}, u32[]{:S(2)}) collective-permute-start(f32[20,128]{1,0:T(8,128)S(1)} %get-tuple-element.29), channel_id=1, source_target_pairs={{0,1},{1,2},{2,3},{3,4},{4,5},{5,6},{6,7},{7,8},{8,9},{9,10},{10,1... | collective-permute-start | bytes 30728 | tf_op jit(solution)/shard_map/ppermute | solution.py:386
  33.2 3.4 %collective-permute-start.1 = (f32[20,128]{1,0:T(8,128)S(1)}, f32[20,128]{1,0:T(8,128)S(1)}, u32[]{:S(2)}, u32[]{:S(2)}) collective-permute-start(f32[20,128]{1,0:T(8,128)S(1)} %get-tuple-element.28), channel_id=1, source_target_pairs={{0,15},{1,0},{2,1},{3,2},{4,3},{5,4},{6,5},{7,6},{8,7},{9,8},{10,9... | collective-permute-start | bytes 30728 | tf_op jit(solution)/shard_map/ppermute | solution.py:386
